TPU v7x, 32 devices: a whole 2x2x4 slice. The times are simulated.
32 devices in a mesh: dp: 4 (over y, x), fsdp: 8 (over z, core).
Axes of the slice: x: 2, y: 2, z: 4, core: 2. Of those that a mesh axis runs over, the one named last changes fastest.
Arguments:
- enc_in: bfloat16 [64, 512, 512], P(('dp', 'fsdp')), may hold values from -6 to 6
- dec_in: bfloat16 [64, 512, 512], P(('dp', 'fsdp')), may hold values from -6 to 6
- bucket: int32 [64], P(('dp', 'fsdp')), may hold values from 0 to 2, as said below
- enc_lengths: int32 [64, 4], P(('dp', 'fsdp')), may hold values from 0 to 512, as said below
- dec_lengths: int32 [64, 4], P(('dp', 'fsdp')), may hold values from 0 to 512, as said below
- pred_ids: int32 [64, 512], P(('dp', 'fsdp')), may hold values from 0 to 522
- running_counts: int32 [523], replicated, may hold values from 0 to 15
- enc_attn_in: bfloat16 [786432], P(('dp', 'fsdp')), may hold values from -0.25 to 0.25
- enc_attn_out: bfloat16 [262144], P(('dp', 'fsdp')), may hold values from -1 to 1
- enc_ff_in: bfloat16 [1048576], P(('dp', 'fsdp')), may hold values from -0.25 to 0.25
- enc_ff_out: bfloat16 [1048576], P(('dp', 'fsdp')), may hold values from -0.125 to 0.125
- enc_norms: bfloat16 [2048], P(('dp', 'fsdp')), may hold values from -1.2 to 1.8
- dec_self_in: bfloat16 [786432], P(('dp', 'fsdp')), may hold values from -0.25 to 0.25
- dec_self_out: bfloat16 [262144], P(('dp', 'fsdp')), may hold values from -1 to 1
- dec_cross_q: bfloat16 [262144], P(('dp', 'fsdp')), may hold values from -0.25 to 0.25
- dec_cross_kv: bfloat16 [524288], P(('dp', 'fsdp')), may hold values from -0.25 to 0.25
- dec_cross_out: bfloat16 [262144], P(('dp', 'fsdp')), may hold values from -1 to 1
- dec_ff_in: bfloat16 [1048576], P(('dp', 'fsdp')), may hold values from -0.25 to 0.25
- dec_ff_out: bfloat16 [1048576], P(('dp', 'fsdp')), may hold values from -0.125 to 0.125
- dec_norms: bfloat16 [3072], P(('dp', 'fsdp')), may hold values from -1.2 to 1.8
- enc_cotangent: bfloat16 [64, 512, 512], P(('dp', 'fsdp')), may hold values from -6 to 6
- dec_cotangent: bfloat16 [64, 512, 512], P(('dp', 'fsdp')), may hold values from -6 to 6
Outputs:
- enc_out: bfloat16 [64, 512, 512], P(('dp', 'fsdp'))
- dec_out: bfloat16 [64, 512, 512], P(('dp', 'fsdp'))
- enc_in_grad: bfloat16 [64, 512, 512], P(('dp', 'fsdp'))
- dec_in_grad: bfloat16 [64, 512, 512], P(('dp', 'fsdp'))
- enc_attn_in_grad: float32 [786432], P(('dp', 'fsdp'))
- enc_attn_out_grad: float32 [262144], P(('dp', 'fsdp'))
- enc_ff_in_grad: float32 [1048576], P(('dp', 'fsdp'))
- enc_ff_out_grad: float32 [1048576], P(('dp', 'fsdp'))
- enc_norms_grad: float32 [2048], P(('dp', 'fsdp'))
- dec_self_in_grad: float32 [786432], P(('dp', 'fsdp'))
- dec_self_out_grad: float32 [262144], P(('dp', 'fsdp'))
- dec_cross_q_grad: float32 [262144], P(('dp', 'fsdp'))
- dec_cross_kv_grad: float32 [524288], P(('dp', 'fsdp'))
- dec_cross_out_grad: float32 [262144], P(('dp', 'fsdp'))
- dec_ff_in_grad: float32 [1048576], P(('dp', 'fsdp'))
- dec_ff_out_grad: float32 [1048576], P(('dp', 'fsdp'))
- dec_norms_grad: float32 [3072], P(('dp', 'fsdp'))
- counts: int32 [523], replicated
Inputs may be any that keep to these rules, and one draw needn't show every extreme that they name: `bucket`: a slot of kind b holds 4 / 2**b sequences, each of up to 512 / 4 * 2**b positions; source and target of a pair share the slot and its sequence number; some slot is of kind 2. `enc_lengths`: for a slot of kind b, entries 0 to 4 / 2**b - 1 are its sequences' lengths, from a quarter of 512 / 4 * 2**b to all of it; the other entries are 0; some slot of kind 2 holds a sequence of all 512 positions. `dec_lengths`: as enc_lengths, for the targets.
All inputs are finite; a program needn't handle non-finite values.
Results may differ from a plain program's by a relative error of at most 0.025.
Values may be sent and summed in bfloat16 or wider, within the bound.
No kernel may reach another device: no remote copies, remote signals or barrier semaphores. Data moves between devices by JAX's collectives and lax.ppermute only.
A program may use at most 192 MiB of HBM per device.

v0:
```python
import functools
import math
import jax
import jax.numpy as jnp
from jax import lax
from jax.experimental import pallas as pl
from jax.experimental.pallas import tpu as pltpu
from jax.sharding import PartitionSpec as P

D = 512
HEAD = 64
FF = 2048
VOCAB = 523
SLOT = 512
SHARDS = 32
BLOCKS = FF // D
EPS = 1e-05
PAIR = 2 * HEAD
PAIRS = D // PAIR
GROUP = 16
MASKED = -(2.0**30)
COST = 0.5
UPPER_MB = 50
BF = jnp.bfloat16
F32 = jnp.float32

SELF_ROWS, SELF_IN, SELF_OUT = 64, 0, 48
FFN_ROWS, FFN_IN, FFN_OUT = 128, 0, 64
CROSS_ROWS, CROSS_Q, CROSS_KV, CROSS_OUT = 64, 0, 16, 48


def nn(left, right):
    return lax.dot_general(left, right, (((1,), (0,)), ((), ())), preferred_element_type=F32)


def nt(left, right):
    return lax.dot_general(left, right, (((1,), (1,)), ((), ())), preferred_element_type=F32)


def wide(ref, start, block):
    first = start + 16 * block
    return ref[:, :, first : first + 16, :].reshape(D, D)


def tall(ref, start, block):
    return ref[4 * block : 4 * block + 4, :, start : start + 64, :].reshape(D, D)


def put_shards(core, refs, lead, rows, shards):
    if len(refs) == 1:
        refs[0][lead, :, rows, :] = shards.astype(BF)
        return
    refs[0][lead, rows, :] = jnp.where(core == 0, shards[:, 0], shards[:, 1]).astype(BF)
    piece = refs[1].shape[1]
    start = rows.start % piece
    refs[1 + rows.start // piece][lead, start : start + rows.stop - rows.start, :] = jnp.where(
        core == 0, shards[:, 1], shards[:, 0]
    ).astype(BF)


def put_wide(core, refs, start, block, value):
    rows = slice(start + 16 * block, start + 16 * block + 16)
    put_shards(core, refs, slice(0, SHARDS // 2), rows, value.reshape(SHARDS // 2, 2, 16, D))


def put_tall(core, refs, start, block, value):
    put_shards(core, refs, slice(4 * block, 4 * block + 4), slice(start, start + 64), value.reshape(4, 2, 64, D))


class Weights:
    def __init__(self, arrays, place, half):
        self.arrays = arrays
        self.place = place
        self.half = half


def weight_copies(pieces, place, half, core, ref, sems, low, high):
    if len(pieces) == 1:
        return [pltpu.make_async_copy(pieces[0].at[:, :, place + low : place + high, :], ref, sems.at[0])]
    copies = []
    for number in range(2):
        first, last = max(low, number * half), min(high, (number + 1) * half)
        if first < last:
            source = slice(place + first - number * half, place + last - number * half)
            for other in range(2):
                copies.append(
                    pltpu.make_async_copy(
                        pieces[2 * number + other].at[:, source, :],
                        ref.at[:, core if other == 0 else 1 - core, first - low : last - low, :],
                        sems.at[2 * number + other],
                    )
                )
    return copies


def on_first_slot(action, copies):
    @pl.when(pl.program_id(0) == 0)
    def _():
        for copy in copies:
            getattr(copy, action)()


def norm_grad_rows(ref, gains_and_shifts):
    rows = jnp.concatenate(gains_and_shifts + [jnp.zeros((8 - len(gains_and_shifts), D), F32)], 0)
    add_up(ref, rows)


def last_slot():
    return pl.program_id(0) == pl.num_programs(0) - 1


def lanes_of(pair):
    return slice(pair * PAIR, (pair + 1) * PAIR)


def normalize(values):
    centered = values - jnp.mean(values, -1, keepdims=True)
    scale = lax.rsqrt(jnp.mean(centered * centered, -1, keepdims=True) + EPS)
    return centered * scale, scale


def norm_backward(grad_normed, unit, scale, gain):
    grad_unit = grad_normed * gain
    first = jnp.mean(grad_unit, -1, keepdims=True)
    second = jnp.mean(grad_unit * unit, -1, keepdims=True)
    grad_gain = jnp.sum(grad_normed * unit, 0, keepdims=True)
    grad_shift = jnp.sum(grad_normed, 0, keepdims=True)
    return scale * (grad_unit - first - unit * second), grad_gain, grad_shift


def gelu_both(hidden):
    size = jnp.abs(hidden)
    ratio = 1.0 / (1.0 + (0.3275911 / math.sqrt(2.0)) * size)
    bell = jnp.exp(-0.5 * hidden * hidden)
    series = 0.5 * 1.061405429
    for factor in (-1.453152027, 1.421413741, -0.284496736, 0.254829592):
        series = series * ratio + 0.5 * factor
    tail = series * ratio * bell
    share = jnp.where(hidden >= 0, 1.0 - tail, tail)
    return hidden * share, share + hidden * bell * (1.0 / math.sqrt(2.0 * math.pi))


def lane_index():
    return lax.broadcasted_iota(jnp.int32, (1, 128), 1)


def query_extra(kind):
    place = lax.broadcasted_iota(jnp.int32, (SLOT, 128), 0)
    lane = lax.broadcasted_iota(jnp.int32, (SLOT, 128), 1)
    return (lax.shift_right_logical(place, kind + 7) == lane).astype(F32).astype(BF)


def key_extra(kind, lengths):
    place = lax.broadcasted_iota(jnp.int32, (SLOT, 128), 0)
    lane = lax.broadcasted_iota(jnp.int32, (SLOT, 128), 1)
    size = lax.shift_left(jnp.int32(128), kind)
    within = place & (size - 1)
    limit = jnp.where(
        lane == 0, lengths[0], jnp.where(lane == 1, lengths[1], jnp.where(lane == 2, lengths[2], lengths[3]))
    )
    allowed = (lax.shift_right_logical(place, kind + 7) == lane) & (within < limit)
    return jnp.where(allowed | (lane >= 4), 0.0, MASKED).astype(BF)


def halves():
    lane = lane_index()
    return ((lane < HEAD).astype(F32).astype(BF), (lane >= HEAD).astype(F32).astype(BF))


def future(rows, columns, first):
    row = lax.broadcasted_iota(jnp.int32, (rows, columns), 0)
    column = lax.broadcasted_iota(jnp.int32, (rows, columns), 1) + first
    return row <= column


def pipelined(items, ahead, start, finish):
    waiting = []
    for number, item in enumerate(items):
        while len(waiting) <= ahead and number + len(waiting) < len(items):
            waiting.append(start(*items[number + len(waiting)]))
        finish(*item, waiting.pop(0))


def attend(query_of, key_of, value_of, store, kind, lengths, causal):
    step = 256
    query_lanes = query_extra(kind)
    key_lanes = key_extra(kind, lengths)
    ones = jnp.ones((HEAD, SLOT), BF)
    mask = halves()
    inputs, parts, sums = {}, {}, {}

    def seen(first):
        return first + step if causal else SLOT

    def start(pair, half, first):
        if pair not in inputs:
            queries = query_of(pair) * BF(HEAD**-0.5)
            inputs[pair] = (queries, jnp.concatenate([key_of(pair), key_lanes], 1), value_of(pair).T)
        queries, keys, _ = inputs[pair]
        own = jnp.concatenate([queries[first : first + step] * mask[half], query_lanes[first : first + step]], 1)
        return nt(keys[: seen(first)], own)

    def finish(pair, half, first, scores):
        values = inputs[pair][2]
        if causal:
            scores = jnp.where(future(seen(first), step, first), scores, MASKED)
        largest = jnp.max(scores, 0, keepdims=True)
        powers = jnp.exp(scores - largest).astype(BF)
        head_values = jnp.concatenate([values[:HEAD], ones] if half == 0 else [ones, values[HEAD:]], 0)
        context = nn(head_values[:, : seen(first)], powers)
        total = context[HEAD : HEAD + 1] if half == 0 else context[0:1]
        parts[pair, half, first] = (context[:HEAD] if half == 0 else context[HEAD:]) * (1.0 / total)
        sums[pair, half, first] = largest + jnp.log(total)
        if half == 1 and first == SLOT - step:
            rows = [jnp.concatenate([parts[pair, side, at] for at in range(0, SLOT, step)], 1) for side in range(2)]
            store(pair, jnp.concatenate(rows, 0).T)

    items = [(pair, half, first) for pair in range(PAIRS) for half in range(2) for first in range(0, SLOT, step)]
    pipelined(items, 4, start, finish)
    spread = [
        jnp.broadcast_to(jnp.concatenate([sums[pair, half, at] for at in range(0, SLOT, step)], 1), (GROUP, SLOT))
        for pair in range(PAIRS)
        for half in range(2)
    ]
    return split(jnp.concatenate(spread, 0).T, 4)


def split(values, first):
    lane = lane_index() % GROUP
    high = values.astype(BF).astype(F32)
    rest = values - high
    middle = rest.astype(BF).astype(F32)
    low = rest - middle
    terms = jnp.where(
        lane == first, high, jnp.where(lane == first + 1, middle, jnp.where(lane == first + 2, low, 0.0))
    )
    return (-terms).astype(BF)


def attend_back(query_of, key_of, value_of, grad_of, contexts, grads, store, logsums, kind, lengths, causal):
    step = 256 if causal else SLOT
    query_lanes = query_extra(kind) + logsums
    key_lanes = key_extra(kind, lengths)
    products = grads.astype(F32) * contexts
    high = products.astype(BF)
    low = (products - high.astype(F32)).astype(BF)
    source = lax.broadcasted_iota(jnp.int32, (D, 128), 0) // HEAD
    target = lax.broadcasted_iota(jnp.int32, (D, 128), 1) // GROUP
    picker = (source == target).astype(F32).astype(BF)
    inner_lanes = split(nn(high, picker) + nn(low, picker), 0)
    lane = lane_index()
    within, group = lane % GROUP, lane // GROUP
    mask = halves()
    inputs, heads, results = {}, {}, {}

    def seen(first):
        return first + step if causal else SLOT

    def start(pair, half, first):
        if pair not in inputs:
            inputs[pair] = (query_of(pair) * BF(HEAD**-0.5), key_of(pair), value_of(pair), grad_of(pair), key_of(pair).T)
        queries, keys, values, grad_context, _ = inputs[pair]
        if (pair, half) not in heads:
            head = 2 * pair + half
            sum_lanes = ((group == head) & (within >= 4) & (within < 7)).astype(F32).astype(BF)
            one_lanes = ((group == head) & (within < 3)).astype(F32).astype(BF)
            heads[pair, half] = (
                jnp.concatenate([keys, key_lanes + sum_lanes], 1),
                jnp.concatenate([queries * mask[half], query_lanes], 1),
                jnp.concatenate([values, jnp.broadcast_to(one_lanes, (SLOT, 128))], 1),
                jnp.concatenate([grad_context * mask[half], inner_lanes], 1),
            )
        left, right, value_left, grad_right = heads[pair, half]
        here = slice(first, first + step)
        return nt(left[: seen(first)], right[here]), nt(value_left[: seen(first)], grad_right[here])

    def finish(pair, half, first, products):
        scores, grad_weights = products
        queries, _, _, grad_context, keys_t = inputs[pair]
        if causal:
            scores = jnp.where(future(seen(first), step, first), scores, MASKED)
        weights = jnp.exp(scores)
        grad_scores = (weights * grad_weights).astype(BF)
        here = slice(first, first + step)
        for_queries = nn(keys_t[half * HEAD : half * HEAD + HEAD, : seen(first)], grad_scores)
        for_keys = nn(grad_scores, queries[here] * mask[half])
        for_values = nn(weights.astype(BF), grad_context[here] * mask[half])
        if seen(first) < SLOT:
            none = jnp.zeros((SLOT - seen(first), PAIR), F32)
            for_keys = jnp.concatenate([for_keys, none], 0)
            for_values = jnp.concatenate([for_values, none], 0)
        results[pair, half, first] = (for_queries, for_keys, for_values)
        if half == 1 and first == SLOT - step:
            places = range(0, SLOT, step)
            rows = [jnp.concatenate([results[pair, side, at][0] for at in places], 1) for side in range(2)]
            keys_sum, values_sum = (
                functools.reduce(jnp.add, [results[pair, side, at][number] for side in range(2) for at in places])
                for number in (1, 2)
            )
            store(
                pair,
                (jnp.concatenate(rows, 0) * HEAD**-0.5).T.astype(BF),
                keys_sum.astype(BF),
                values_sum.astype(BF),
            )

    items = [(pair, half, first) for pair in range(PAIRS) for half in range(2) for first in range(0, SLOT, step)]
    pipelined(items, 2 if causal else 1, start, finish)


def lengths_at(ref, slot):
    return [ref[slot, entry] for entry in range(4)]


def at(ref, start):
    return lambda pair: ref[0, :, start + pair * PAIR : start + (pair + 1) * PAIR]


def add_up(ref, value):
    ref[...] = jnp.where(pl.program_id(0) == 0, 0.0, ref[...]) + value


def project_kernel(
    me_ref,
    x_refs,
    weights,
    norm_refs,
    qkv_refs,
    enc_ref,
    enc_sems,
    dec_ref,
    dec_sems,
    *,
    places,
    halves_of,
    slots,
):
    step = pl.program_id(0)
    held = ((enc_ref, enc_sems), (dec_ref, dec_sems))
    sides = []
    for side, (ref, sems) in enumerate(held):
        sides.append(
            weight_copies(
                weights[side], places[side], halves_of[side], me_ref[4], ref, sems, SELF_IN, SELF_OUT
            )
        )
    on_first_slot("start", sides[0] + sides[1])
    for side, (ref, _) in enumerate(held):

        @pl.when((step >= side * slots) & (step < (side + 1) * slots))
        def _(side=side, ref=ref):
            unit, _ = normalize(x_refs[side][0].astype(F32))
            normed = (unit * norm_refs[side][0:1] + norm_refs[side][1:2]).astype(BF)

            @pl.when(step == side * slots)
            def _():
                for copy in sides[side]:
                    copy.wait()

            for block in range(3):
                qkv_refs[side][0, :, block * D : (block + 1) * D] = nn(normed, wide(ref, 0, block)).astype(BF)


def keep_context(context_ref, rest_ref):
    def store(pair, context):
        high = context.astype(BF)
        context_ref[0, :, lanes_of(pair)] = high
        rest_ref[0, :, lanes_of(pair)] = (context - high.astype(F32)).astype(BF)

    return store


def self_attend_kernel(
    kind_ref,
    lengths_ref,
    me_ref,
    x_ref,
    qkv_ref,
    w,
    out_ref,
    context_ref,
    rest_ref,
    sums_ref,
    weights_ref,
    sems,
    *,
    place,
    half,
    causal,
):
    slot = pl.program_id(0)
    copies = weight_copies(w, place, half, me_ref[4], weights_ref, sems, SELF_OUT, SELF_ROWS)
    on_first_slot("start", copies)
    sums_ref[0] = attend(
        at(qkv_ref, 0),
        at(qkv_ref, D),
        at(qkv_ref, 2 * D),
        keep_context(context_ref, rest_ref),
        kind_ref[slot],
        lengths_at(lengths_ref, slot),
        causal,
    )
    on_first_slot("wait", copies)
    out_ref[0] = x_ref[0].astype(F32) + nn(context_ref[0], wide(weights_ref, 0, 0))


def ffn_forward_kernel(
    me_ref, r_ref, w, norm_ref, out_ref, active_ref, slope_ref, weights_ref, sems, *, place, half
):
    copies = weight_copies(w, place, half, me_ref[4], weights_ref, sems, 0, FFN_ROWS)
    on_first_slot("start", copies)
    values = r_ref[0]
    unit, _ = normalize(values)
    normed = (unit * norm_ref[2:3] + norm_ref[3:4]).astype(BF)
    totals = []
    on_first_slot("wait", copies)

    def finish(block, hidden):
        active, slope = gelu_both(hidden)
        active = active.astype(BF)
        active_ref[0, :, block * D : (block + 1) * D] = active
        slope_ref[0, :, block * D : (block + 1) * D] = slope.astype(BF)
        totals.append(nn(active, tall(weights_ref, FFN_OUT, block)))

    pipelined(
        [(block,) for block in range(BLOCKS)], 1, lambda block: nn(normed, wide(weights_ref, FFN_IN, block)), finish
    )
    total = functools.reduce(jnp.add, totals, values)
    out_ref[0] = total.astype(BF)


def ffn_back(grad_out, unit, scale, normed, gain, kept, w_ref, sums_ref):
    low = grad_out.astype(BF)
    normed_t = normed.T
    parts = []

    def start(block):
        return nt(low, tall(w_ref, FFN_OUT, block)), kept(block, False)

    def finish(block, products):
        grad_active, begun = products
        active, slope = kept(block, True) if begun is None else begun()
        grad_hidden = (grad_active * slope).astype(BF)
        add_up(sums_ref.at[1, block], nn(active.T, low))
        add_up(sums_ref.at[0, block], nn(normed_t, grad_hidden))
        parts.append(nt(grad_hidden, wide(w_ref, FFN_IN, block)))

    pipelined([(block,) for block in range(BLOCKS)], 1, start, finish)
    grad, grad_gain, grad_shift = norm_backward(functools.reduce(jnp.add, parts), unit, scale, gain)
    return grad_out + grad, grad_gain, grad_shift


def ffn_put(core, sums_ref, grads):
    @pl.when(last_slot())
    def _():
        for block in range(BLOCKS):
            put_wide(core, grads, FFN_IN, block, sums_ref[0, block])
            put_tall(core, grads, FFN_OUT, block, sums_ref[1, block])


def ffn_backward_kernel(
    me_ref,
    grad_out_ref,
    r_ref,
    active_ref,
    slope_ref,
    w,
    norm_ref,
    grad_ref,
    grads,
    norm_grad_ref,
    weights_ref,
    sems,
    sums_ref,
    *,
    place,
    half,
):
    copies = weight_copies(w, place, half, me_ref[4], weights_ref, sems, 0, FFN_ROWS)
    on_first_slot("start", copies)
    unit, scale = normalize(r_ref[0])
    gain = norm_ref[2:3]
    normed = (unit * gain + norm_ref[3:4]).astype(BF)
    on_first_slot("wait", copies)
    grad, grad_gain, grad_shift = ffn_back(
        grad_out_ref[0],
        unit,
        scale,
        normed,
        gain,
        lambda block, late: (
            (
                active_ref[0, :, block * D : (block + 1) * D],
                slope_ref[0, :, block * D : (block + 1) * D].astype(F32),
            )
            if late
            else None
        ),
        weights_ref,
        sums_ref,
    )
    grad_ref[0] = grad
    norm_grad_rows(norm_grad_ref, [grad_gain, grad_shift])
    ffn_put(me_ref[4], sums_ref, grads)


def attend_back_kernel(
    kind_ref,
    lengths_ref,
    me_ref,
    grad_out_ref,
    q_ref,
    kv_ref,
    context_ref,
    rest_ref,
    sums_in_ref,
    w,
    proj_ref,
    weights_ref,
    sems,
    low_ref,
    *,
    place,
    half,
    causal,
    start,
    key_at,
):
    slot = pl.program_id(0)
    copies = weight_copies(w, place, half, me_ref[4], weights_ref, sems, start, start + 16)
    on_first_slot("start", copies)
    on_first_slot("wait", copies)
    low_ref[0] = nt(grad_out_ref[0].astype(BF), wide(weights_ref, 0, 0)).astype(BF)

    def store(pair, grad_query, grad_key, grad_value):
        for number, value in enumerate((grad_query, grad_key, grad_value)):
            proj_ref[0, :, number * D + pair * PAIR : number * D + (pair + 1) * PAIR] = value

    attend_back(
        at(q_ref, 0),
        at(kv_ref, key_at),
        at(kv_ref, key_at + D),
        at(low_ref, 0),
        context_ref[0].astype(F32) + rest_ref[0].astype(F32),
        low_ref[0],
        store,
        sums_in_ref[0],
        kind_ref[slot],
        lengths_at(lengths_ref, slot),
        causal,
    )


def upper_kernel(
    kind_ref,
    lengths_ref,
    me_ref,
    r_ref,
    memory_ref,
    enc_cotangent_ref,
    dec_cotangent_ref,
    w_cross,
    w_ff,
    norm_ref,
    out_ref,
    grad_ref,
    memory_grad_ref,
    ff_grads,
    cross_grads,
    norm_grad_ref,
    cross_ref,
    cross_sems,
    ff_ref,
    ff_sems,
    qkv_ref,
    context_ref,
    low_ref,
    proj_ref,
    second_ref,
    ff_sums_ref,
    sums_ref,
    *,
    cross_place,
    cross_half,
    ff_place,
    ff_half,
):
    slot = pl.program_id(0)
    core = me_ref[4]
    copies = weight_copies(w_cross, cross_place, cross_half, core, cross_ref, cross_sems, 0, CROSS_ROWS)
    ff_copies = weight_copies(w_ff, ff_place, ff_half, core, ff_ref, ff_sems, 0, FFN_ROWS)
    on_first_slot("start", copies + ff_copies)
    kind, lengths = kind_ref[slot], lengths_at(lengths_ref, slot)
    unit, scale = normalize(r_ref[0])
    gain = norm_ref[2:3]
    normed = (unit * gain + norm_ref[3:4]).astype(BF)
    memory = memory_ref[0]
    on_first_slot("wait", copies)
    qkv_ref[0, :, :D] = nn(normed, wide(cross_ref, CROSS_Q, 0)).astype(BF)
    for block in range(2):
        qkv_ref[0, :, (block + 1) * D : (block + 2) * D] = nn(memory, wide(cross_ref, CROSS_KV, block)).astype(BF)

    def keep(pair, context):
        context_ref[:, lanes_of(pair)] = context

    logsums = attend(at(qkv_ref, 0), at(qkv_ref, D), at(qkv_ref, 2 * D), keep, kind, lengths, False)
    second = r_ref[0] + nn(context_ref[...].astype(BF), wide(cross_ref, CROSS_OUT, 0))

    ff_unit, ff_scale = normalize(second)
    ff_gain = norm_ref[4:5]
    ff_normed = (ff_unit * ff_gain + norm_ref[5:6]).astype(BF)
    on_first_slot("wait", ff_copies)
    totals = []

    def kept(block, _):
        hidden = nn(ff_normed, wide(ff_ref, FFN_IN, block))

        def rest():
            active, slope = gelu_both(hidden)
            active = active.astype(BF)
            totals.append(nn(active, tall(ff_ref, FFN_OUT, block)))
            return active, slope

        return rest

    grad_second, ff_gain_grad, ff_shift_grad = ffn_back(
        dec_cotangent_ref[0].astype(F32), ff_unit, ff_scale, ff_normed, ff_gain, kept, ff_ref, ff_sums_ref
    )
    out_ref[0] = functools.reduce(jnp.add, totals, second).astype(BF)
    second_ref[...] = grad_second

    low = second_ref[...].astype(BF)
    add_up(sums_ref.at[3], nn(context_ref[...].astype(BF).T, low))
    low_ref[0] = nt(low, wide(cross_ref, CROSS_OUT, 0)).astype(BF)

    def store(pair, grad_query, grad_key, grad_value):
        for number, value in enumerate((grad_query, grad_key, grad_value)):
            proj_ref[number, :, lanes_of(pair)] = value

    attend_back(
        at(qkv_ref, 0),
        at(qkv_ref, D),
        at(qkv_ref, 2 * D),
        at(low_ref, 0),
        context_ref[...],
        low_ref[0],
        store,
        logsums,
        kind,
        lengths,
        False,
    )
    unit, scale = normalize(r_ref[0])
    normed_t = (unit * gain + norm_ref[3:4]).astype(BF).T
    memory_t = memory_ref[0].T
    add_up(sums_ref.at[0], nn(normed_t, proj_ref[0]))
    add_up(sums_ref.at[1], nn(memory_t, proj_ref[1]))
    add_up(sums_ref.at[2], nn(memory_t, proj_ref[2]))
    memory_grad_ref[0] = (
        enc_cotangent_ref[0].astype(F32)
        + nt(proj_ref[1], wide(cross_ref, CROSS_KV, 0))
        + nt(proj_ref[2], wide(cross_ref, CROSS_KV, 1))
    )
    grad, grad_gain, grad_shift = norm_backward(nt(proj_ref[0], wide(cross_ref, CROSS_Q, 0)), unit, scale, gain)
    grad_ref[0] = second_ref[...] + grad
    norm_grad_rows(norm_grad_ref, [grad_gain, grad_shift, ff_gain_grad, ff_shift_grad])
    ffn_put(core, ff_sums_ref, ff_grads)

    @pl.when(last_slot())
    def _():
        put_wide(core, cross_grads, CROSS_Q, 0, sums_ref[0])
        put_wide(core, cross_grads, CROSS_KV, 0, sums_ref[1])
        put_wide(core, cross_grads, CROSS_KV, 1, sums_ref[2])
        put_wide(core, cross_grads, CROSS_OUT, 0, sums_ref[3])


def self_weight_kernel(
    me_ref, grad_out_ref, x_ref, context_ref, proj_ref, norm_ref, grads, sums_ref
):
    unit, _ = normalize(x_ref[0].astype(F32))
    normed_t = (unit * norm_ref[0:1] + norm_ref[1:2]).astype(BF).T
    for block in range(3):
        add_up(sums_ref.at[block], nn(normed_t, proj_ref[0, :, block * D : (block + 1) * D]))
    add_up(sums_ref.at[3], nn(context_ref[0].T, grad_out_ref[0].astype(BF)))

    @pl.when(last_slot())
    def _():
        core = me_ref[4]
        for block in range(3):
            put_wide(core, grads, SELF_IN, block, sums_ref[block])
        put_wide(core, grads, SELF_OUT, 0, sums_ref[3])


def self_rows_kernel(
    me_ref,
    grad_out_ref,
    x_ref,
    proj_ref,
    w,
    norm_ref,
    grad_ref,
    norm_grad_ref,
    weights_ref,
    sems,
    *,
    place,
    half,
):
    copies = weight_copies(w, place, half, me_ref[4], weights_ref, sems, SELF_IN, SELF_OUT)
    on_first_slot("start", copies)
    unit, scale = normalize(x_ref[0].astype(F32))
    on_first_slot("wait", copies)
    grad_normed = None
    for block in range(3):
        part = nt(proj_ref[0, :, block * D : (block + 1) * D], wide(weights_ref, 0, block))
        grad_normed = part if grad_normed is None else grad_normed + part
    grad, grad_gain, grad_shift = norm_backward(grad_normed, unit, scale, norm_ref[0:1])
    grad_ref[0] = (grad_out_ref[0] + grad).astype(BF)
    norm_grad_rows(norm_grad_ref, [grad_gain, grad_shift])


def per_slot(*shape):
    return pl.BlockSpec((1,) + shape, lambda slot: (slot,) + (0,) * len(shape))


def whole_block(*shape):
    return pl.BlockSpec(shape, lambda slot: (0,) * len(shape))


def scalars():
    return pl.BlockSpec(memory_space=pltpu.SMEM)


def in_place():
    return pl.BlockSpec(memory_space=pl.ANY)


def in_vmem():
    return pl.BlockSpec(memory_space=pltpu.VMEM)


class Order:
    def __init__(self):
        self.token = ()

    def call(self, kernel, name, steps, ins, outs, scratch, args, megabytes, us):
        leaf = lambda out: isinstance(out[0], pl.BlockSpec)
        shaped = lambda out: pltpu.HBM(*out[1:3]) if out[3:] else jax.ShapeDtypeStruct(*out[1:])
        specs = [out[0] if leaf(out) else tuple(part[0] for part in out) for out in outs]
        shapes = [shaped(out) if leaf(out) else tuple(shaped(part) for part in out) for out in outs]
        place = len(ins) + len(outs)

        def body(before, *refs):
            refs[place][...] = jnp.zeros((8, 128), F32)
            kernel(*refs[:place], *refs[place + 1 :])

        *results, token = pl.pallas_call(
            body,
            name=name,
            grid=(steps,),
            in_specs=[tuple(in_place() for _ in self.token)] + ins,
            out_specs=specs + [whole_block(8, 128)],
            out_shape=shapes + [jax.ShapeDtypeStruct((8, 128), F32)],
            scratch_shapes=scratch,
            cost_estimate=pl.CostEstimate(flops=int(COST * us * 1.15e9), bytes_accessed=1 << 16, transcendentals=0),
            compiler_params=pltpu.CompilerParams(
                vmem_limit_bytes=megabytes << 20, dimension_semantics=("arbitrary",)
            ),
        )(self.token, *args)
        self.token = (token,)
        return results


def slot_array(slots, width, dtype, to_hbm=False):
    return (per_slot(SLOT, width), (slots, SLOT, width), dtype) + (("hbm",) if to_hbm else ())


def stay(*arrays):
    return tuple(pltpu.with_memory_space_constraint(array, pltpu.HBM) for array in arrays)


def stay_own(weights):
    if len(weights.arrays) == 1:
        return stay(*weights.arrays)
    return tuple(stay(array)[0] if number % 2 == 0 else array for number, array in enumerate(weights.arrays))


def grad_group(rows, parted, pieces=1):
    def once(*shape):
        spec = pl.BlockSpec(shape, lambda slot: (0,) * len(shape), pipeline_mode=pl.Buffered(1))
        return (spec, shape, BF)

    if not parted:
        return (once(SHARDS // 2, 2, rows, D),)
    return (once(SHARDS // 2, rows, D),) + (once(SHARDS // 2, rows // pieces, D),) * pieces


NORM_GRADS = (whole_block(8, D), (8, D), F32)


def weight_scratch(rows):
    return [pltpu.VMEM((SHARDS // 2, 2, rows, D), BF), pltpu.SemaphoreType.DMA((4,))]


def bound(kernel, weights, **options):
    return functools.partial(kernel, place=weights.place, half=weights.half, **options)


def held(weights):
    return tuple(in_place() for _ in weights.arrays)


def project(order, me, rows, weights, norms):
    slots = rows[0].shape[0]

    def turn(side, width):
        first = side * slots
        return pl.BlockSpec(
            (1, SLOT, width), lambda step: (jnp.minimum(jnp.maximum(step - first, 0), slots - 1), 0, 0)
        )

    return order.call(
        functools.partial(
            project_kernel,
            places=tuple(part.place for part in weights),
            halves_of=tuple(part.half for part in weights),
            slots=slots,
        ),
        "project",
        2 * slots,
        [
            scalars(),
            tuple(turn(side, D) for side in range(2)),
            tuple(held(part) for part in weights),
            tuple(whole_block(*part.shape) for part in norms),
        ],
        [tuple((turn(side, 3 * D), (slots, SLOT, 3 * D), BF, "hbm") for side in range(2))],
        weight_scratch(SELF_OUT - SELF_IN) * 2,
        (me, stay(*rows), tuple(stay_own(part) for part in weights), tuple(norms)),
        20,
        8,
    )[0]


def self_attend(order, kinds, lengths, me, rows, qkv, weights, causal, name):
    slots = rows.shape[0]
    return order.call(
        bound(self_attend_kernel, weights, causal=causal),
        name,
        slots,
        [scalars(), scalars(), scalars(), per_slot(SLOT, D), per_slot(SLOT, 3 * D), held(weights)],
        [slot_array(slots, D, F32, True)] + [slot_array(slots, D, BF, True)] * 2 + [slot_array(slots, 128, BF, True)],
        weight_scratch(SELF_ROWS - SELF_OUT),
        (kinds, lengths, me, *stay(rows, qkv), stay_own(weights)),
        14,
        10,
    )


def ffn_forward(order, me, rows, weights, norms):
    slots = rows.shape[0]
    return order.call(
        bound(ffn_forward_kernel, weights),
        "ffn_forward",
        slots,
        [scalars(), per_slot(SLOT, D), held(weights), whole_block(*norms.shape)],
        [slot_array(slots, D, BF, True), slot_array(slots, FF, BF, True), slot_array(slots, FF, BF, True)],
        weight_scratch(FFN_ROWS),
        (me, *stay(rows), stay_own(weights), norms),
        24,
        16,
    )


def ffn_backward(order, me, grad_out, rows, active, slope, weights, norms, parted):
    slots = rows.shape[0]
    return order.call(
        bound(ffn_backward_kernel, weights),
        "ffn_backward",
        slots,
        [
            scalars(),
            per_slot(SLOT, D),
            per_slot(SLOT, D),
            per_slot(SLOT, FF),
            per_slot(SLOT, FF),
            held(weights),
            whole_block(*norms.shape),
        ],
        [slot_array(slots, D, F32), grad_group(FFN_ROWS, parted), NORM_GRADS],
        weight_scratch(FFN_ROWS) + [pltpu.VMEM((2, BLOCKS, D, D), F32)],
        (me, *stay(grad_out, rows, active, slope), stay_own(weights), norms),
        30,
        22,
    )


def attend_backward(order, kinds, lengths, me, grad_out, q, kv, kept, weights, causal, start, key_at, name):
    slots = grad_out.shape[0]
    return order.call(
        bound(attend_back_kernel, weights, causal=causal, start=start, key_at=key_at),
        name,
        slots,
        [scalars(), scalars(), scalars(), per_slot(SLOT, D)]
        + [per_slot(SLOT, part.shape[-1]) for part in (q, kv)]
        + [per_slot(SLOT, D), per_slot(SLOT, D), per_slot(SLOT, 128), held(weights)],
        [slot_array(slots, 3 * D, BF)],
        weight_scratch(16) + [pltpu.VMEM((1, SLOT, D), BF)],
        (kinds, lengths, me, grad_out, *stay(q, kv, *kept), stay_own(weights)),
        18,
        16,
    )[0]


def upper(order, kinds, lengths, me, rows, memory, enc_cotangent, dec_cotangent, w_cross, w_ff, norms, parted):
    slots = rows.shape[0]
    return order.call(
        functools.partial(
            upper_kernel, cross_place=w_cross.place, cross_half=w_cross.half, ff_place=w_ff.place, ff_half=w_ff.half
        ),
        "upper_decoder",
        slots,
        [scalars(), scalars(), scalars()]
        + [per_slot(SLOT, D)] * 4
        + [held(w_cross), held(w_ff), whole_block(*norms.shape)],
        [
            slot_array(slots, D, BF, True),
            slot_array(slots, D, F32),
            slot_array(slots, D, F32, True),
            grad_group(FFN_ROWS, parted),
            grad_group(CROSS_ROWS, parted),
            NORM_GRADS,
        ],
        weight_scratch(CROSS_ROWS)
        + weight_scratch(FFN_ROWS)
        + [
            pltpu.VMEM((1, SLOT, 3 * D), BF),
            pltpu.VMEM((SLOT, D), F32),
            pltpu.VMEM((1, SLOT, D), BF),
            pltpu.VMEM((3, SLOT, D), BF),
            pltpu.VMEM((SLOT, D), F32),
            pltpu.VMEM((2, BLOCKS, D, D), F32),
            pltpu.VMEM((4, D, D), F32),
        ],
        (
            kinds,
            lengths,
            me,
            *stay(rows, memory, enc_cotangent, dec_cotangent),
            stay_own(w_cross),
            stay_own(w_ff),
            norms,
        ),
        UPPER_MB,
        60,
    )


def self_weights(order, me, grad_out, rows, context, proj, norms, parted, name):
    slots = rows.shape[0]
    return order.call(
        self_weight_kernel,
        name,
        slots,
        [scalars()] + [per_slot(SLOT, D)] * 3 + [per_slot(SLOT, 3 * D), whole_block(*norms.shape)],
        [grad_group(SELF_ROWS, parted, 4)],
        [pltpu.VMEM((4, D, D), F32)],
        (me, grad_out, *stay(rows, context), proj, norms),
        14,
        8,
    )[0]


def self_rows(order, me, grad_out, rows, proj, weights, norms, name):
    slots = rows.shape[0]
    return order.call(
        bound(self_rows_kernel, weights),
        name,
        slots,
        [scalars(), per_slot(SLOT, D), per_slot(SLOT, D), per_slot(SLOT, 3 * D), held(weights), whole_block(*norms.shape)],
        [slot_array(slots, D, BF), NORM_GRADS],
        weight_scratch(SELF_OUT - SELF_IN),
        (me, *stay(grad_out, rows), proj, stay_own(weights), norms),
        16,
        7,
    )


def axis_sizes(mesh):
    dp, fsdp = mesh.shape["dp"], mesh.shape["fsdp"]
    core = 2 if fsdp % 2 == 0 else 1
    side = math.isqrt(dp)
    first, second = (side, side) if side * side == dp else (dp, 1)
    return (first, second, fsdp // core, core)


AXES = ("dp", "fsdp")
CUBE = (2, 2, 4, 2)
A_BIT, B_BIT, HIGH_BIT, LOW_BIT, CORE_BIT = 16, 8, 4, 2, 1


def swapped(values, bit):
    return lax.ppermute(values, AXES, [(device, device ^ bit) for device in range(SHARDS)])


def moved(values, sizes, axis, shift):
    stride = math.prod(sizes[axis + 1 :])
    pairs = []
    for device in range(math.prod(sizes)):
        place = device // stride % sizes[axis]
        pairs.append((device, device + ((place + shift) % sizes[axis] - place) * stride))
    return lax.ppermute(values, AXES, pairs)


def sum_everywhere(values, sizes):
    for axis in (3, 1, 0, 2):
        total = values
        for shift in range(1, sizes[axis]):
            total = total + moved(values, sizes, axis, shift)
        values = total
    return values


def packed(flat, rows, columns, devices):
    part = flat.reshape(rows // devices, columns // D, D)
    return jnp.swapaxes(part, 0, 1).reshape(-1, D)


def unpacked(part, rows, columns, devices):
    return jnp.swapaxes(part.reshape(columns // D, rows // devices, D), 0, 1).reshape(-1)


SELF_SHAPES = ((D, 3 * D), (D, D))
FFN_SHAPES = ((D, FF), (FF, D))
CROSS_SHAPES = ((D, D), (D, 2 * D), (D, D))


def rows_of(shapes, devices=SHARDS):
    return sum(rows * columns for rows, columns in shapes) // D // devices


def rows_in(groups):
    return sum(rows_of(shapes) for shapes in groups)


def join_copy_kernel(me_ref, sources, results, sems, *, plan):
    copies = []
    for result, (source, _, bit, axis) in zip(results, plan):
        for other, ref in enumerate(sources[source]):
            place = me_ref[bit] if other == 0 else 1 - me_ref[bit]
            target = result.at[place] if axis == 0 else result.at[:, place]
            copies.append(pltpu.make_async_copy(ref, target, sems.at[len(copies)]))
    for copy in copies:
        copy.start()
    for copy in copies:
        copy.wait()


def join_kernel(me_ref, sources, results, *, plan):
    for result, (source, rows, bit, axis) in zip(results, plan):
        for other, ref in enumerate(sources[source]):
            place = me_ref[bit] if other == 0 else 1 - me_ref[bit]
            if axis == 0:
                result[place] = ref[...]
            else:
                for lead in range(2):
                    result[lead, place] = ref[lead] if rows is None else ref[lead, rows]


def join(order, me, name, sources, plan, to_hbm=False):
    outs = []
    for source, rows, _, axis in plan:
        shape = sources[source][0].shape
        count = shape[-2] if rows is None else rows.stop - rows.start
        shape = (2, *shape[:-2], count, D) if axis == 0 else (shape[0], 2, *shape[1:-2], count, D)
        outs.append((in_place(), shape, BF, "hbm") if to_hbm else (in_vmem(), shape, BF))
    return order.call(
        functools.partial(join_copy_kernel if to_hbm else join_kernel, plan=plan),
        name,
        1,
        [scalars(), [(in_vmem(), in_vmem())] * len(sources)],
        [tuple(outs)],
        [pltpu.SemaphoreType.DMA((2 * len(plan),))] if to_hbm else [],
        (me, sources),
        20,
        1,
    )[0]


def pack_kernel(me_ref, flats, extra, out_ref, *scratch, plan):
    for flat, wide_ref, (rows, blocks, places) in zip(flats, scratch, plan):
        wide_ref[...] = flat[...].astype(F32)
        for block, place in enumerate(places):
            for chunk in range(4):
                part = wide_ref[pl.ds(4 * block + chunk, rows, stride=4 * blocks), :]
                out_ref[place : place + rows, 128 * chunk : 128 * chunk + 128] = part.astype(BF)
    if extra:
        place = out_ref.shape[0] - 16
        out_ref[place:, :] = jnp.broadcast_to(extra[0][...], (16, D))


def pack_groups(order, me, name, groups, extra):
    counts = [rows_of([shape for _, shape in group]) for group in groups]
    total = sum(counts)
    flats, plan, scratch, before = [], [], [], 0
    for group, count in zip(groups, counts):
        first = 0
        for flat, (rows, columns) in group:
            rows, blocks = rows // SHARDS, columns // D
            places = []
            for block in range(blocks):
                at = first + block * rows
                places.append(before + at if at < count // 2 else total // 2 + before + at - count // 2)
            first += rows * blocks
            flats.append(flat.reshape(-1, 128))
            plan.append((rows, blocks, tuple(places)))
            scratch.append(pltpu.VMEM((rows * blocks * 4, 128), F32))
        before += count // 2
    rows = total + (0 if extra is None else 16)
    return order.call(
        functools.partial(pack_kernel, plan=plan),
        name + "_pack",
        1,
        [
            scalars(),
            tuple(whole_block(*flat.shape) for flat in flats),
            () if extra is None else (whole_block(*extra.shape),),
        ],
        [(in_vmem(), (rows, D), BF)],
        scratch,
        (me, tuple(flats), () if extra is None else (extra,)),
        20,
        1,
    )[0]


def gather_cube(order, me, name, groups, spans, extra, results):
    halves_of = [rows_of([shape for _, shape in group]) // 2 for group in groups]
    count = sum(halves_of)
    values = pack_groups(order, me, name, groups, extra)
    total = values.shape[0]
    yield
    got = swapped(values, HIGH_BIT)
    yield
    (values,) = join(order, me, name + "_join_1", [(values, got)], [(0, None, 2, 0)])
    got = swapped(values, LOW_BIT)
    yield
    plan, members, place = [], [], 0
    for span in spans:
        members.append([halves_of.pop(0) for _ in range(span)])
        end = place + sum(members[-1])
        plan.append((0, slice(place, end), 3, 1))
        plan.append((0, slice(count + place, total if end == count else count + end), 3, 1))
        place = end
    parts = join(order, me, name + "_join_2", [(values, got)], plan)
    for number, held_halves in enumerate(members):
        last = extra is not None and number == len(members) - 1
        results.append(
            Exchange(
                lambda kept, number=number, held_halves=held_halves, last=last: gather_rest(
                    order, me, f"{name}_{number}", parts[2 * number], parts[2 * number + 1], held_halves, last, kept
                )
            )
        )
    yield


def gather_rest(order, me, name, one, two, halves_of, extra, results):
    got = swapped(one, B_BIT), swapped(two, A_BIT)
    yield
    one, two = join(
        order, me, name + "_join_3", [(one, got[0]), (two, got[1])], [(0, None, 1, 0), (1, None, 0, 0)]
    )
    got = swapped(one, A_BIT), swapped(two, B_BIT)
    yield
    one, two = join(
        order, me, name + "_join_4", [(one, got[0]), (two, got[1])], [(0, None, 0, 0), (1, None, 1, 1)], True
    )
    got = swapped(one, CORE_BIT), swapped(two, CORE_BIT)
    arrays = tuple(part.reshape(SHARDS // 2, -1, D) for part in (one, got[0], two, got[1]))
    place = 0
    for half in halves_of:
        results.append(Weights(arrays, place, half))
        place += half
    if extra:
        own, other = arrays[2][:, place], arrays[3][:, place]
        lines = jnp.where(me[4] == 0, jnp.stack([own, other], 1), jnp.stack([other, own], 1))
        results.append(lines.reshape(SHARDS, D))
    yield


def gather_plain(groups, spans, extra, devices, results):
    if devices == SHARDS:
        parts = [packed(flat, *shape, SHARDS) for group in groups for flat, shape in group]
        whole = lax.all_gather(jnp.concatenate(parts, 0), AXES, axis=0)
    else:
        parts = []
        for flat, shape in [pair for group in groups for pair in group]:
            full = lax.all_gather(flat, AXES, axis=0, tiled=True)
            full = full.reshape(SHARDS, shape[0] // SHARDS, shape[1] // D, D)
            parts.append(jnp.swapaxes(full, 1, 2).reshape(SHARDS, -1, D))
        whole = jnp.concatenate(parts, 1)
    whole = whole.reshape(SHARDS // 2, 2, -1, D)
    place, left = 0, list(groups)
    for span in spans:
        results.append(Exchange())
        for _ in range(span):
            count = rows_of([shape for _, shape in left.pop(0)])
            results[-1].results.append(Weights((whole,), place, count // 2))
            place += count
    if extra is not None:
        results[-1].results.append(lax.all_gather(extra[0], AXES, axis=0))


CARRIED = 48


def carry(ref, first, values):
    high = values.astype(BF).astype(F32)
    rest = values - high
    middle = rest.astype(BF).astype(F32)
    for number, term in enumerate((high, middle, rest - middle)):
        ref[first + 16 * number : first + 16 * number + 16, :] = term.astype(BF)


def carried(ref, first):
    terms = [ref[first + 16 * number : first + 16 * number + 16, :].astype(F32) for number in range(3)]
    return terms[0] + (terms[1] + terms[2])


def slab(ref, index, rows):
    return ref.at[pl.ds(pl.multiple_of(index * rows, rows), rows), :]


def first_sum_kernel(me_ref, keeps, gots, small, send_one, keep_one, send_two, keep_two, *small_out):
    a, b = me_ref[0], me_ref[1]
    total = keep_one.shape[0] // 8
    place = 0
    for keep, pieces in zip(keeps, gots):
        half = keep.shape[3] // 2
        size = min(pieces[0].shape[3], half)
        for first in range(0, 2 * half, size):
            got = pieces[first // pieces[0].shape[3]]
            at = first % pieces[0].shape[3]
            rows, source = slice(first, first + size), slice(at, at + size)
            here = place + first % half
            for other in range(2):
                for z in range(4):
                    target = slice((4 * other + z) * total + here, (4 * other + z) * total + here + size)
                    if first < half:
                        for ref, pick in ((send_one, 1 - b), (keep_one, b)):
                            ref[target] = keep[other, pick, z, rows] + got[other, pick, z, source]
                    else:
                        for ref, pick in ((send_two, 1 - a), (keep_two, a)):
                            ref[target] = keep[pick, other, z, rows] + got[pick, other, z, source]
        place += half
    if small:
        values = small[0][...] + small[1][...]
        small_out[0][...] = values
        carry(send_one, 8 * total, values)


def second_sum_kernel(me_ref, keep_one, got_one, keep_two, got_two, small, send_a, kept_a, send_b, kept_b, *small_out):
    a, b = me_ref[0], me_ref[1]
    rows = kept_a.shape[0]
    for keep, got, outs, mine in ((keep_one, got_one, (send_a, kept_a), a), (keep_two, got_two, (send_b, kept_b), b)):
        for ref, pick in zip(outs, (1 - mine, mine)):
            ref[:rows] = slab(keep, pick, rows)[...] + slab(got, pick, rows)[...]
    if small:
        values = small[0][...] + carried(got_one, 2 * rows)
        small_out[0][...] = values
        carry(send_a, rows, values)


def third_sum_kernel(me_ref, keep_one, got_one, keep_two, got_two, small, send, keep, *small_out):
    z = me_ref[3]
    half = keep_one.shape[0] // 4
    for high in range(2):
        for ref, pick in ((send, 1 - z), (keep, z)):
            first = 2 * high * half
            ref[first : first + half] = slab(keep_one, 2 * high + pick, half)[...] + slab(got_one, 2 * high + pick, half)[...]
            ref[first + half : first + 2 * half] = (
                slab(keep_two, 2 * high + pick, half)[...] + slab(got_two, 2 * high + pick, half)[...]
            )
    if small:
        values = small[0][...] + carried(got_one, 4 * half)
        small_out[0][...] = values
        carry(send, 4 * half, values)


def fourth_sum_kernel(me_ref, keep, got, small, send, kept, *small_out):
    z = me_ref[2]
    rows = kept.shape[0]
    for ref, pick in ((send, 1 - z), (kept, z)):
        ref[:rows] = slab(keep, pick, rows)[...] + slab(got, pick, rows)[...]
    if small:
        values = small[0][...] + carried(got, 2 * rows)
        small_out[0][...] = values
        carry(send, rows, values)


def scatter_cube(order, me, name, groups, small, results):
    got = [tuple(swapped(part, CORE_BIT) for part in pair[1:]) for pair, _ in groups]
    small = () if small is None else (small, swapped(small, CORE_BIT))
    extra = CARRIED if small else 0
    yield
    keeps = tuple(pair[0].reshape(2, 2, 4, -1, D) for pair, _ in groups)
    got = tuple(tuple(part.reshape(2, 2, 4, -1, D) for part in parts) for parts in got)
    half = sum(rows_of(shapes) for _, shapes in groups) // 2

    def call(kernel, number, rows, *args):
        outs = [(in_vmem(), (count, D), BF) for count in rows] + [(in_vmem(), (16, D), F32)] * bool(small)
        ins = jax.tree.map(lambda _: in_vmem(), list(args) + [small])
        parts = order.call(kernel, f"{name}_sum_{number}", 1, [scalars()] + ins, outs, [], (me, *args, small), 20, 1)
        return parts[: len(rows)], tuple(parts[len(rows) :])

    (send_one, keep_one, send_two, keep_two), small = call(
        first_sum_kernel, 1, (8 * half + extra, 8 * half, 8 * half, 8 * half), keeps, got
    )
    got = swapped(send_one, B_BIT), swapped(send_two, A_BIT)
    yield
    (send_one, keep_one, send_two, keep_two), small = call(
        second_sum_kernel, 2, (4 * half + extra, 4 * half, 4 * half, 4 * half), keep_one, got[0], keep_two, got[1]
    )
    got = swapped(send_one, A_BIT), swapped(send_two, B_BIT)
    yield
    (send, keep), small = call(
        third_sum_kernel, 3, (4 * half + extra, 4 * half), keep_one, got[0], keep_two, got[1]
    )
    got = swapped(send, LOW_BIT)
    yield
    (send, keep), small = call(fourth_sum_kernel, 4, (2 * half + extra, 2 * half), keep, got)
    last = (keep, swapped(send, HIGH_BIT))
    yield
    plan, outs, place = [], [], 0
    for _, shapes in groups:
        count, first = rows_of(shapes), 0
        for rows, columns in shapes:
            rows, blocks = rows // SHARDS, columns // D
            places = []
            for block in range(blocks):
                at = first + block * rows
                places.append(place + at if at < count // 2 else half + place + at - count // 2)
            first += rows * blocks
            plan.append((rows, blocks, tuple(places)))
            shape = (rows * blocks * 4, 128)
            outs.append((whole_block(*shape), shape, F32))
        place += count // 2
    flat, *sums = order.call(
        functools.partial(finish_kernel, plan=plan),
        name + "_finish",
        1,
        [scalars(), tuple(in_vmem() for _ in last), tuple(in_vmem() for _ in small)],
        [tuple(outs)] + [(in_vmem(), (16, D), F32)] * bool(small),
        [],
        (me, last, small),
        20,
        1,
    )
    results.extend(part.reshape(-1) for part in flat)
    results.extend(sums)
    yield


def finish_kernel(me_ref, parts, small, outs, *small_out, plan):
    for out, (rows, blocks, places) in zip(outs, plan):
        for block, place in enumerate(places):
            part = functools.reduce(jnp.add, [ref[place : place + rows, :].astype(F32) for ref in parts])
            for chunk in range(4):
                out[pl.ds(4 * block + chunk, rows, stride=4 * blocks), :] = part[:, 128 * chunk : 128 * chunk + 128]
    if small:
        small_out[0][...] = small[0][...] + carried(parts[1], parts[0].shape[0])


def unpack_group(rows, shapes):
    results, first = [], 0
    for shape in shapes:
        count = rows_of((shape,))
        results.append(unpacked(rows[first : first + count], *shape, SHARDS))
        first += count
    return results


def scatter_plain(grads, shapes, devices):
    if devices == SHARDS:
        own = lax.psum_scatter(grads.reshape(-1, D), AXES, scatter_dimension=0, tiled=True)
        return unpack_group(own.astype(F32), shapes)
    grads = grads.reshape(SHARDS, -1, D)
    results, first = [], 0
    for rows, columns in shapes:
        count = rows_of(((rows, columns),))
        part = grads[:, first : first + count].reshape(SHARDS, columns // D, rows // SHARDS, D)
        flat = jnp.swapaxes(part, 1, 2).reshape(devices, -1)
        results.append(lax.psum_scatter(flat, AXES, scatter_dimension=0, tiled=True).reshape(-1).astype(F32))
        first += count
    return results


class Exchange:
    def __init__(self, steps=None):
        self.results = []
        self.steps = None if steps is None else steps(self.results)

    def part(self, number):
        return self.results[number]

    def go(self, count=1):
        if self.steps is not None:
            for _ in range(count):
                next(self.steps)


def count_kernel(kind_ref, lengths_ref, ids_ref, out_ref, *, slots):
    totals = [jnp.zeros((1, 128), F32) for _ in range(8)]
    place = lax.broadcasted_iota(jnp.int32, (SLOT, 128), 0)
    lane = lax.broadcasted_iota(jnp.int32, (SLOT, 128), 1).astype(F32)
    for slot in range(slots):
        kind = kind_ref[slot]
        sequence = lax.shift_right_logical(place, kind + 7)
        within = place & (lax.shift_left(jnp.int32(128), kind) - 1)
        limit = jnp.zeros_like(place)
        for entry in range(4):
            limit = jnp.where(sequence == entry, lengths_ref[slot, entry], limit)
        ids = jnp.broadcast_to(ids_ref[slot : slot + 1].astype(F32), (128, SLOT)).T
        ids = jnp.where(within < limit, ids, -1.0)
        for chunk in range((VOCAB + 127) // 128):
            hits = jnp.where(ids == lane + 128.0 * chunk, 1.0, 0.0)
            totals[chunk] = totals[chunk] + jnp.sum(hits, 0, keepdims=True)
    out_ref[...] = jnp.concatenate([jnp.concatenate(totals[:4], 1), jnp.concatenate(totals[4:], 1)], 0)


def count_live(order, kinds, lengths, ids):
    slots = ids.shape[0]
    return order.call(
        functools.partial(count_kernel, slots=slots),
        "count",
        1,
        [scalars(), scalars(), in_vmem()],
        [(in_vmem(), (2, D), F32)],
        [],
        (kinds, lengths, ids),
        8,
        1,
    )[0]


def local(
    sizes,
    enc_in,
    dec_in,
    bucket,
    enc_lengths,
    dec_lengths,
    pred_ids,
    running_counts,
    enc_attn_in,
    enc_attn_out,
    enc_ff_in,
    enc_ff_out,
    enc_norms,
    dec_self_in,
    dec_self_out,
    dec_cross_q,
    dec_cross_kv,
    dec_cross_out,
    dec_ff_in,
    dec_ff_out,
    dec_norms,
    enc_cotangent,
    dec_cotangent,
):
    devices = math.prod(sizes)
    cube = sizes == CUBE
    index = lax.axis_index("dp") * lax.axis_size("fsdp") + lax.axis_index("fsdp")
    if cube:
        me = jnp.stack([index >> 4 & 1, index >> 3 & 1, index >> 2 & 1, index >> 1 & 1, index & 1]).astype(jnp.int32)
    else:
        me = jnp.zeros((5,), jnp.int32)

    order = Order()

    def gather(name, groups, spans, extra=None):
        if cube:
            return Exchange(lambda results: gather_cube(order, me, name, groups, spans, extra, results))
        exchange = Exchange()
        gather_plain(groups, spans, extra, devices, exchange.results)
        return exchange

    def scatter(name, *groups, small=None):
        if cube:
            return Exchange(lambda results: scatter_cube(order, me, name, groups, small, results))
        exchange = Exchange()
        for (grads,), shapes in groups:
            exchange.results.extend(scatter_plain(grads, shapes, devices))
        if small is not None:
            exchange.results.append(sum_everywhere(small, sizes))
        return exchange

    enc_count, dec_count = enc_norms.shape[0], dec_norms.shape[0]
    both = jnp.concatenate([enc_norms, dec_norms])
    norm_part = jnp.pad(both[None, :], ((0, 0), (0, D - both.shape[0])))
    enc_self_group = list(zip((enc_attn_in, enc_attn_out), SELF_SHAPES))
    dec_self_group = list(zip((dec_self_in, dec_self_out), SELF_SHAPES))
    enc_ff_group = list(zip((enc_ff_in, enc_ff_out), FFN_SHAPES))
    cross_group = list(zip((dec_cross_q, dec_cross_kv, dec_cross_out), CROSS_SHAPES))
    dec_ff_group = list(zip((dec_ff_in, dec_ff_out), FFN_SHAPES))
    first = gather("self", [dec_self_group, enc_self_group], [2], norm_part)
    ffn = gather("ffn", [enc_ff_group], [1])
    late = gather("late", [cross_group, dec_ff_group], [2])
    first.go(2)
    ffn.go()
    late.go()
    counted = count_live(order, bucket, dec_lengths, pred_ids)
    first.go(2)
    self_chain = first.part(0)
    self_chain.go()
    ffn.go(2)
    self_chain.go()
    late.go()
    ffn.go()
    ffn_chain = ffn.part(0)
    self_chain.go()
    ffn_chain.go()
    dec_self_w, enc_self_w, norm_lines = self_chain.results
    enc_norm = norm_lines[:, :enc_count].reshape(4, D).astype(F32)
    dec_norm = norm_lines[:, enc_count : enc_count + dec_count].reshape(6, D).astype(F32)

    enc_qkv, dec_qkv = project(order, me, (enc_in, dec_in), (enc_self_w, dec_self_w), (enc_norm, dec_norm))
    late.go()
    ffn_chain.go()
    attended, *enc_kept = self_attend(order, bucket, enc_lengths, me, enc_in, enc_qkv, enc_self_w, False, "enc_attend")
    late.go()
    late_chain = late.part(0)
    late_chain.go()
    ffn_chain.go()
    first_out, *dec_kept = self_attend(order, bucket, dec_lengths, me, dec_in, dec_qkv, dec_self_w, True, "dec_attend")
    late_chain.go()
    (enc_ff_w,) = ffn_chain.results
    memory, active, slope = ffn_forward(order, me, attended, enc_ff_w, enc_norm)
    late_chain.go()
    cross_w, dec_ff_w = late_chain.results
    decoded, grad_first, grad_memory, dec_ff_grads, cross_grads, upper_norm_g = upper(
        order,
        bucket,
        enc_lengths,
        me,
        first_out,
        memory,
        enc_cotangent,
        dec_cotangent,
        cross_w,
        dec_ff_w,
        dec_norm,
        cube,
    )
    fifth = scatter("dec", (dec_ff_grads, FFN_SHAPES), (cross_grads, CROSS_SHAPES))
    fifth.go()
    grad_attended, enc_ff_grads, enc_ffn_norm_g = ffn_backward(
        order, me, grad_memory, attended, active, slope, enc_ff_w, enc_norm, cube
    )
    fifth.go()
    enc_proj = attend_backward(
        order,
        bucket,
        enc_lengths,
        me,
        grad_attended,
        enc_qkv,
        enc_qkv,
        enc_kept,
        enc_self_w,
        False,
        SELF_OUT,
        D,
        "enc_attend_back",
    )
    fifth.go()
    enc_self_grads = self_weights(
        order, me, grad_attended, enc_in, enc_kept[0], enc_proj, enc_norm, cube, "enc_self_weights"
    )
    sixth = scatter("enc", (enc_ff_grads, FFN_SHAPES), (enc_self_grads, SELF_SHAPES))
    sixth.go()
    dec_proj = attend_backward(
        order,
        bucket,
        dec_lengths,
        me,
        grad_first,
        dec_qkv,
        dec_qkv,
        dec_kept,
        dec_self_w,
        True,
        SELF_OUT,
        D,
        "dec_attend_back",
    )
    fifth.go()
    sixth.go()
    grad_enc_in, enc_self_norm_g = self_rows(
        order, me, grad_attended, enc_in, enc_proj, enc_self_w, enc_norm, "enc_self_rows"
    )
    fifth.go()
    grad_dec_in, dec_self_norm_g = self_rows(order, me, grad_first, dec_in, dec_proj, dec_self_w, dec_norm, "dec_self_rows")
    sixth.go()
    small = jnp.concatenate(
        [enc_self_norm_g[:2], enc_ffn_norm_g[:2], dec_self_norm_g[:2], upper_norm_g[:4], counted, jnp.zeros((4, D), F32)],
        0,
    )
    dec_self_grads = self_weights(
        order, me, grad_first, dec_in, dec_kept[0], dec_proj, dec_norm, cube, "dec_self_weights"
    )
    seventh = scatter("self", (dec_self_grads, SELF_SHAPES), small=small)
    seventh.go()
    fifth.go()
    sixth.go()
    seventh.go()
    sixth.go()
    seventh.go()
    seventh.go()
    sixth.go()
    seventh.go()
    seventh.go()
    dec_ff_in_g, dec_ff_out_g, cross_q_g, cross_kv_g, cross_out_g = fifth.results
    enc_ff_in_g, enc_ff_out_g, enc_attn_in_g, enc_attn_out_g = sixth.results
    dec_self_in_g, dec_self_out_g, small = seventh.results

    enc_norm_own = lax.dynamic_slice(small[:4].reshape(-1), (index * enc_count,), (enc_count,))
    dec_norm_own = lax.dynamic_slice(small[4:10].reshape(-1), (index * dec_count,), (dec_count,))
    counts = running_counts + small[10:12].reshape(-1)[:VOCAB].astype(jnp.int32)
    return (
        memory,
        decoded,
        grad_enc_in,
        grad_dec_in,
        enc_attn_in_g,
        enc_attn_out_g,
        enc_ff_in_g,
        enc_ff_out_g,
        enc_norm_own,
        dec_self_in_g,
        dec_self_out_g,
        cross_q_g,
        cross_kv_g,
        cross_out_g,
        dec_ff_in_g,
        dec_ff_out_g,
        dec_norm_own,
        counts,
    )


def solution(mesh):
    rows = P(AXES, None, None)
    pair = P(AXES, None)
    flat = P(AXES)
    return jax.shard_map(
        functools.partial(local, axis_sizes(mesh)),
        mesh=mesh,
        in_specs=(rows, rows, flat, pair, pair, pair, P()) + (flat,) * 13 + (rows, rows),
        out_specs=(rows,) * 4 + (flat,) * 13 + (P(),),
        check_vma=False,
    )
```

profile of v0, /device:TPU:0, one launch (start us, length us, event | category | flops | bytes accessed | tf_op | source)
XLA Modules:
  0.0 329.4 jit_solution(5143632921001334077)
XLA Ops:
  5.2 4.1 %collective-permute-start = (bf16[144,512]{1,0:T(8,128)(2,1)S(1)}, bf16[144,512]{1,0:T(8,128)(2,1)S(1)}, u32[]{:S(2)}, u32[]{:S(2)}) collective-permute-start(bf16[144,512]{1,0:T(8,128)(2,1)S(1)} %get-tuple-element.182.refs_1__0__0_), channel_id=1, source_target_pairs={{0,4},{1,5},{2,6},{3,7},{4,0},{5,1},{6,2},{7,3},{8,12},{9,13},{10,... | collective-permute-start | bytes 442376 | tf_op jit(solution)/shard_map/ppermute | solution.py:1003
  11.9 4.5 %collective-permute-done.refs_1__0__1_ = bf16[144,512]{1,0:T(8,128)(2,1)S(1)} collective-permute-done((bf16[144,512]{1,0:T(8,128)(2,1)S(1)}, bf16[144,512]{1,0:T(8,128)(2,1)S(1)}, u32[]{:S(2)}, u32[]{:S(2)}) %collective-permute-start) | collective-permute-done | bytes 147488 | tf_op jit(solution)/shard_map/ppermute | solution.py:1003
  17.7 7.5 %collective-permute-done.1.refs_1__0__1_ = bf16[2,144,512]{2,1,0:T(8,128)(2,1)S(1)} collective-permute-done((bf16[2,144,512]{2,1,0:T(8,128)(2,1)S(1)}, bf16[2,144,512]{2,1,0:T(8,128)(2,1)S(1)}, u32[]{:S(2)}, u32[]{:S(2)}) %collective-permute-start.1) | collective-permute-done | bytes 294944 | tf_op jit(solution)/shard_map/ppermute | solution.py:1003
  28.6 3.3 %collective-permute-start.2 = (bf16[128,512]{1,0:T(8,128)(2,1)S(1)}, bf16[128,512]{1,0:T(8,128)(2,1)S(1)}, u32[]{:S(2)}, u32[]{:S(2)}) collective-permute-start(bf16[128,512]{1,0:T(8,128)(2,1)S(1)} %get-tuple-element.186.refs_1__0__0_), channel_id=1, source_target_pairs={{0,4},{1,5},{2,6},{3,7},{4,0},{5,1},{6,2},{7,3},{8,12},{9,13},{10,... | collective-permute-start | bytes 393224 | tf_op jit(solution)/shard_map/ppermute | solution.py:1003
  31.9 5.4 %collective-permute-done.2.refs_1__0__1_ = bf16[128,512]{1,0:T(8,128)(2,1)S(1)} collective-permute-done((bf16[128,512]{1,0:T(8,128)(2,1)S(1)}, bf16[128,512]{1,0:T(8,128)(2,1)S(1)}, u32[]{:S(2)}, u32[]{:S(2)}) %collective-permute-start.2) | collective-permute-done | bytes 131104 | tf_op jit(solution)/shard_map/ppermute | solution.py:1003
  40.3 6.1 %collective-permute-done.5.refs_1__0__1_ = bf16[2,128,512]{2,1,0:T(8,128)(2,1)S(1)} collective-permute-done((bf16[2,128,512]{2,1,0:T(8,128)(2,1)S(1)}, bf16[2,128,512]{2,1,0:T(8,128)(2,1)S(1)}, u32[]{:S(2)}, u32[]{:S(2)}) %collective-permute-start.5) | collective-permute-done | bytes 262176 | tf_op jit(solution)/shard_map/ppermute | solution.py:1003
  47.0 4.8 %collective-permute-done.6.refs_1__0__1_ = bf16[2,2,2,64,512]{4,3,2,1,0:T(8,128)(2,1)S(1)} collective-permute-done((bf16[2,2,2,64,512]{4,3,2,1,0:T(8,128)(2,1)S(1)}, bf16[2,2,2,64,512]{4,3,2,1,0:T(8,128)(2,1)S(1)}, u32[]{:S(2)}, u32[]{:S(2)}) %collective-permute-start.6) | collective-permute-done | bytes 524320 | tf_op jit(solution)/shard_map/ppermute | solution.py:1003
  51.8 2.6 collective-permute-done.7.refs_1__1__1_
  54.3 2.0 self_0_join_4.1
  61.1 9.8 %project.1 = (bf16[2,512,1536]{2,1,0:T(8,128)(2,1)}, bf16[2,512,1536]{2,1,0:T(8,128)(2,1)}, f32[8,128]{1,0:T(8,128)S(1)}) custom-call(f32[8,128]{1,0:T(8,128)S(1)} %get-tuple-element.195.before_0_, s32[5]{0:T(128)S(1)} %stack.29.refs_0_.refs_2_, bf16[2,512,512]{2,1,0:T(8,128)(2,1)} %refs_2_.7, bf16[2,512,512]{2,1,0:T(8,128)(2,1)} %refs_2_.9, ...), custom_call_target="tpu_custom_call" | custom-call | flops 4600000000 | bytes 65536 | tf_op jit(solution)/shard_map/project/pallas_call | solution.py:757
  72.0 2.5 collective-permute-start.13
  80.3 10.4 %enc_attend.1 = (f32[2,512,512]{2,1,0:T(8,128)}, bf16[2,512,512]{2,1,0:T(8,128)(2,1)}, bf16[2,512,512]{2,1,0:T(8,128)(2,1)}, bf16[2,512,128]{2,1,0:T(8,128)(2,1)}, f32[8,128]{1,0:T(8,128)S(1)}) custom-call(f32[8,128]{1,0:T(8,128)S(1)} %get-tuple-element.203.before_0_, s32[2]{0:T(128)S(1)} %copy-done.23, s32[2,4]{1,0:T(2,128)S(1)} %copy-done.21, ...), custom_call_target="tpu_custom_call" | custom-call | flops 5750000128 | bytes 65536 | tf_op jit(solution)/shard_map/enc_attend/pallas_call | solution.py:757
  91.4 1.9 ffn_0_join_4.1
  95.8 8.3 %dec_attend.1 = (f32[2,512,512]{2,1,0:T(8,128)}, bf16[2,512,512]{2,1,0:T(8,128)(2,1)}, bf16[2,512,512]{2,1,0:T(8,128)(2,1)}, bf16[2,512,128]{2,1,0:T(8,128)(2,1)}, f32[8,128]{1,0:T(8,128)S(1)}) custom-call(f32[8,128]{1,0:T(8,128)S(1)} %get-tuple-element.210.before_0_, s32[2]{0:T(128)S(1)} %copy-done.23, s32[2,4]{1,0:T(2,128)S(1)} %copy-done.22, ...), custom_call_target="tpu_custom_call" | custom-call | flops 5750000128 | bytes 65536 | tf_op jit(solution)/shard_map/dec_attend/pallas_call | solution.py:757
  107.9 15.1 %ffn_forward.1 = (bf16[2,512,512]{2,1,0:T(8,128)(2,1)}, bf16[2,512,2048]{2,1,0:T(8,128)(2,1)}, bf16[2,512,2048]{2,1,0:T(8,128)(2,1)}, f32[8,128]{1,0:T(8,128)S(1)}) custom-call(f32[8,128]{1,0:T(8,128)S(1)} %get-tuple-element.215.before_0_, s32[5]{0:T(128)S(1)} %stack.29.refs_0_.refs_2_, f32[2,512,512]{2,1,0:T(8,128)} %get-tuple-element.216.refs_1_.refs_2_, ...), custom_call_target="tpu_custom_call" | custom-call | flops 9200000000 | bytes 65536 | tf_op jit(solution)/shard_map/ffn_forward/pallas_call | solution.py:757
  123.1 2.1 collective-permute-done.20.refs_1__0__1_
  125.4 2.2 late_0_join_4.1
  128.2 3.1 collective-permute-done.22
  131.3 2.2 collective-permute-done.23
  134.8 51.9 %upper_decoder.1 = (bf16[2,512,512]{2,1,0:T(8,128)(2,1)}, f32[2,512,512]{2,1,0:T(8,128)}, f32[2,512,512]{2,1,0:T(8,128)}, bf16[16,128,512]{2,1,0:T(8,128)(2,1)},...) custom-call(f32[8,128]{1,0:T(8,128)S(1)} %get-tuple-element.223.befo, ...), custom_call_target="tpu_custom_call" | custom-call | flops 34500001792 | bytes 65536 | tf_op jit(solution)/shard_map/upper_decoder/pallas_call | solution.py:757
  187.3 16.5 %ffn_backward.1 = (f32[2,512,512]{2,1,0:T(8,128)S(1)}, bf16[16,128,512]{2,1,0:T(8,128)(2,1)S(1)}, bf16[16,128,512]{2,1,0:T(8,128)(2,1)S(1)}, f32[8,512]{1,0:T(8,128)S(1)}, f32[8,128]{1,0:T(8,128)S(1)}) custom-call(f32[8,128]{1,0:T(8,128)S(1)} %get-tuple-element.228.before_0_, s32[5]{0:T(128)S(1)} %stack.29.refs_0_.refs_2_, ...), custom_call_target="tpu_custom_call" | custom-call | flops 12650000384 | bytes 65536 | tf_op jit(solution)/shard_map/ffn_backward/pallas_call | solution.py:757
  207.2 17.1 %enc_attend_back.1 = (bf16[2,512,1536]{2,1,0:T(8,128)(2,1)S(1)}, f32[8,128]{1,0:T(8,128)S(1)}) custom-call(f32[8,128]{1,0:T(8,128)S(1)} %get-tuple-element.237.before_0_, s32[2]{0:T(128)S(1)} %copy-done.23, s32[2,4]{1,0:T(2,128)S(1)} %copy-done.21, s32[5]{0:T(128)S(1)} %stack.29.refs_0_.refs_2_, f32[2,512,512]{2,1,0:T(8,128)S(1)} %get-tuple-element.238.refs_3_.refs_1_, ...), custom_call_target="tpu_custom_call" | custom-call | flops 9200000000 | bytes 65536 | tf_op jit(solution)/shard_map/enc_attend_back/pallas_call | solution.py:757
  228.9 5.3 %enc_self_weights.1 = (bf16[16,64,512]{2,1,0:T(8,128)(2,1)S(1)}, bf16[16,16,512]{2,1,0:T(8,128)(2,1)S(1)}, bf16[16,16,512]{2,1,0:T(8,128)(2,1)S(1)}, bf16[16,16,...) custom-call(f32[8,128]{1,0:T(8,128)S(1)} %get-tuple-element.247.before_0_, ...), custom_call_target="tpu_custom_call" | custom-call | flops 4600000000 | bytes 65536 | tf_op jit(solution)/shard_map/enc_self_weights/pallas_call | solution.py:757
  237.5 14.5 %dec_attend_back.1 = (bf16[2,512,1536]{2,1,0:T(8,128)(2,1)S(1)}, f32[8,128]{1,0:T(8,128)S(1)}) custom-call(f32[8,128]{1,0:T(8,128)S(1)} %get-tuple-element.249.before_0_, s32[2]{0:T(128)S(1)} %copy-done.23, s32[2,4]{1,0:T(2,128)S(1)} %copy-done.22, s32[5]{0:T(128)S(1)} %stack.29.refs_0_.refs_2_, f32[2,512,512]{2,1,0:T(8,128)S(1)} %copy-done.24, ...), custom_call_target="tpu_custom_call" | custom-call | flops 9200000000 | bytes 65536 | tf_op jit(solution)/shard_map/dec_attend_back/pallas_call | solution.py:757
  256.2 6.5 %enc_self_rows.1 = (bf16[2,512,512]{2,1,0:T(8,128)(2,1)}, f32[8,512]{1,0:T(8,128)S(1)}, f32[8,128]{1,0:T(8,128)S(1)}) custom-call(f32[8,128]{1,0:T(8,128)S(1)} %get-tuple-element.267.before_0_, s32[5]{0:T(128)S(1)} %stack.29.refs_0_.refs_2_, f32[2,512,512]{2,1,0:T(8,128)} %copy-done.26, bf16[2,512,512]{2,1,0:T(8,128)(2,1)} %refs_2_.7, ...), custom_call_target="tpu_custom_call" | custom-call | flops 4024999936 | bytes 65536 | tf_op jit(solution)/shard_map/enc_self_rows/pallas_call | solution.py:757
  266.6 6.4 %dec_self_rows.1 = (bf16[2,512,512]{2,1,0:T(8,128)(2,1)}, f32[8,512]{1,0:T(8,128)S(1)}, f32[8,128]{1,0:T(8,128)S(1)}) custom-call(f32[8,128]{1,0:T(8,128)S(1)} %get-tuple-element.272.before_0_, s32[5]{0:T(128)S(1)} %stack.29.refs_0_.refs_2_, f32[2,512,512]{2,1,0:T(8,128)} %get-tuple-element.250.refs_3_.refs_1_, bf16[2,512,512]{2,1,0:T(8,128)(2,1)} %refs_2_.9, ...), custom_call_target="tpu_custom_call" | custom-call | flops 4024999936 | bytes 65536 | tf_op jit(solution)/shard_map/dec_self_rows/pallas_call | solution.py:757
  277.5 6.2 %dec_self_weights.1 = (bf16[16,64,512]{2,1,0:T(8,128)(2,1)S(1)}, bf16[16,16,512]{2,1,0:T(8,128)(2,1)}, bf16[16,16,512]{2,1,0:T(8,128)(2,1)}, bf16[16,16,512]{2,1...) custom-call(f32[8,128]{1,0:T(8,128)S(1)} %get-tuple-element.280.before_0_, ...), custom_call_target="tpu_custom_call" | custom-call | flops 4600000000 | bytes 65536 | tf_op jit(solution)/shard_map/dec_self_weights/pallas_call | solution.py:757
  294.4 7.2 %collective-permute-done.46.refs_2_ = bf16[384,512]{1,0:T(8,128)(2,1)S(1)} collective-permute-done((bf16[384,512]{1,0:T(8,128)(2,1)S(1)}, bf16[384,512]{1,0:T(8,128)(2,1)S(1)}, u32[]{:S(2)}, u32[]{:S(2)}) %collective-permute-start.46) | collective-permute-done | bytes 393248 | tf_op jit(solution)/shard_map/ppermute | solution.py:1003
  304.7 1.9 collective-permute-start.51
  310.9 5.0 %collective-permute-done.51.refs_1__1_ = bf16[192,512]{1,0:T(8,128)(2,1)S(1)} collective-permute-done((bf16[192,512]{1,0:T(8,128)(2,1)S(1)}, bf16[192,512]{1,0:T(8,128)(2,1)S(1)}, u32[]{:S(2)}, u32[]{:S(2)}) %collective-permute-start.51) | collective-permute-done | bytes 196640 | tf_op jit(solution)/shard_map/ppermute | solution.py:1003
  317.9 2.3 collective-permute-start.53
  320.2 5.9 %collective-permute-done.53.refs_1__1_ = bf16[112,512]{1,0:T(8,128)(2,1)S(1)} collective-permute-done((bf16[112,512]{1,0:T(8,128)(2,1)S(1)}, bf16[112,512]{1,0:T(8,128)(2,1)S(1)}, u32[]{:S(2)}, u32[]{:S(2)}) %collective-permute-start.53) | collective-permute-done | bytes 114720 | tf_op jit(solution)/shard_map/ppermute | solution.py:1003
  (208 shorter events, 83.0 us)
Async XLA Ops:
  5.2 11.1 %collective-permute-start = (bf16[144,512]{1,0:T(8,128)(2,1)S(1)}, bf16[144,512]{1,0:T(8,128)(2,1)S(1)}, u32[]{:S(2)}, u32[]{:S(2)}) collective-permute-start(bf16[144,512]{1,0:T(8,128)(2,1)S(1)} %get-tuple-element.182.refs_1__0__0_), channel_id=1, source_target_pairs={{0,4},{1,5},{2,6},{3,7},{4,0},{5,1},{6,2},{7,3},{8,12},{9,13},{10,... | collective-permute-start | bytes 442376 | tf_op jit(solution)/shard_map/ppermute | solution.py:1003
  25.7 12.2 %collective-permute-start.4 = (bf16[2,2,80,512]{3,2,1,0:T(8,128)(2,1)S(1)}, bf16[2,2,80,512]{3,2,1,0:T(8,128)(2,1)S(1)}, u32[]{:S(2)}, u32[]{:S(2)}) collective-permute-start(bf16[2,2,80,512]{3,2,1,0:T(8,128)(2,1)S(1)} %get-tuple-element.189.refs_1__1__0_), channel_id=1, source_target_pairs={{0,16},{1,17},{2,18},{3,19},{4,20},{5,21},{6,22},{7,23},{8,24},{9,... | collective-permute-start | bytes 983048 | tf_op jit(solution)/shard_map/ppermute | solution.py:1003
  38.5 15.8 %collective-permute-start.7 = (bf16[2,2,2,80,512]{4,3,2,1,0:T(8,128)(2,1)S(1)}, bf16[2,2,2,80,512]{4,3,2,1,0:T(8,128)(2,1)S(1)}, u32[]{:S(2)}, u32[]{:S(2)}) collective-permute-start(bf16[2,2,2,80,512]{4,3,2,1,0:T(8,128)(2,1)S(1)} %get-tuple-element.194.refs_1__1__0_), channel_id=1, source_target_pairs={{0,8},{1,9},{2,10},{3,11},{4,12},{5,13},{6,14},{7,15},{8,0},{9,1},... | collective-permute-start | bytes 1966088 | tf_op jit(solution)/shard_map/ppermute | solution.py:1003
  39.1 12.6 %collective-permute-start.6 = (bf16[2,2,2,64,512]{4,3,2,1,0:T(8,128)(2,1)S(1)}, bf16[2,2,2,64,512]{4,3,2,1,0:T(8,128)(2,1)S(1)}, u32[]{:S(2)}, u32[]{:S(2)}) collective-permute-start(bf16[2,2,2,64,512]{4,3,2,1,0:T(8,128)(2,1)S(1)} %get-tuple-element.193.refs_1__0__0_), channel_id=1, source_target_pairs={{0,16},{1,17},{2,18},{3,19},{4,20},{5,21},{6,22},{7,23},{8,24},{9,... | collective-permute-start | bytes 1572872 | tf_op jit(solution)/shard_map/ppermute | solution.py:1003
  56.9 14.1 %collective-permute-start.10 = (bf16[192,512]{1,0:T(8,128)(2,1)S(1)}, bf16[192,512]{1,0:T(8,128)(2,1)}, u32[]{:S(2)}, u32[]{:S(2)}) collective-permute-start(bf16[192,512]{1,0:T(8,128)(2,1)S(1)} %get-tuple-element.199.refs_1__0__0_), channel_id=1, source_target_pairs={{0,4},{1,5},{2,6},{3,7},{4,0},{5,1},{6,2},{7,3},{8,12},{9,13},{10,... | collective-permute-start | bytes 589832 | tf_op jit(solution)/shard_map/ppermute | solution.py:1003
  56.9 17.7 %collective-permute-start.11 = (bf16[2,2,64,512]{3,2,1,0:T(8,128)(2,1)S(1)}, bf16[2,2,64,512]{3,2,1,0:T(8,128)(2,1)S(1)}, u32[]{:S(2)}, u32[]{:S(2)}) collective-permute-start(bf16[2,2,64,512]{3,2,1,0:T(8,128)(2,1)S(1)} %get-tuple-element.201.refs_1__0__0_), channel_id=1, source_target_pairs={{0,8},{1,9},{2,10},{3,11},{4,12},{5,13},{6,14},{7,15},{8,0},{9,1},... | collective-permute-start | bytes 786440 | tf_op jit(solution)/shard_map/ppermute | solution.py:1003
  58.0 17.3 %collective-permute-start.12 = (bf16[2,2,64,512]{3,2,1,0:T(8,128)(2,1)S(1)}, bf16[2,2,64,512]{3,2,1,0:T(8,128)(2,1)}, u32[]{:S(2)}, u32[]{:S(2)}) collective-permute-start(bf16[2,2,64,512]{3,2,1,0:T(8,128)(2,1)S(1)} %get-tuple-element.202.refs_1__1__0_), channel_id=1, source_target_pairs={{0,16},{1,17},{2,18},{3,19},{4,20},{5,21},{6,22},{7,23},{8,24},{9,... | collective-permute-start | bytes 786440 | tf_op jit(solution)/shard_map/ppermute | solution.py:1003
  72.0 18.7 %collective-permute-start.13 = (bf16[2,192,512]{2,1,0:T(8,128)(2,1)S(1)}, bf16[2,192,512]{2,1,0:T(8,128)(2,1)S(1)}, u32[]{:S(2)}, u32[]{:S(2)}) collective-permute-start(bf16[2,192,512]{2,1,0:T(8,128)(2,1)S(1)} %get-tuple-element.206.refs_1__0__0_), channel_id=1, source_target_pairs={{0,2},{1,3},{2,0},{3,1},{4,6},{5,7},{6,4},{7,5},{8,10},{9,11},{10,... | collective-permute-start | bytes 1179656 | tf_op jit(solution)/shard_map/ppermute | solution.py:1003
  77.3 14.1 %collective-permute-start.14 = (bf16[2,2,2,64,512]{4,3,2,1,0:T(8,128)(2,1)S(1)}, bf16[2,2,2,64,512]{4,3,2,1,0:T(8,128)(2,1)S(1)}, u32[]{:S(2)}, u32[]{:S(2)}) collective-permute-start(bf16[2,2,2,64,512]{4,3,2,1,0:T(8,128)(2,1)S(1)} %get-tuple-element.208.refs_1__0__0_), channel_id=1, source_target_pairs={{0,16},{1,17},{2,18},{3,19},{4,20},{5,21},{6,22},{7,23},{8,24},{9,... | collective-permute-start | bytes 1572872 | tf_op jit(solution)/shard_map/ppermute | solution.py:1003
  78.8 12.5 %collective-permute-start.15 = (bf16[2,2,2,64,512]{4,3,2,1,0:T(8,128)(2,1)S(1)}, bf16[2,2,2,64,512]{4,3,2,1,0:T(8,128)(2,1)S(1)}, u32[]{:S(2)}, u32[]{:S(2)}) collective-permute-start(bf16[2,2,2,64,512]{4,3,2,1,0:T(8,128)(2,1)S(1)} %get-tuple-element.209.refs_1__1__0_), channel_id=1, source_target_pairs={{0,8},{1,9},{2,10},{3,11},{4,12},{5,13},{6,14},{7,15},{8,0},{9,1},... | collective-permute-start | bytes 1572872 | tf_op jit(solution)/shard_map/ppermute | solution.py:1003
  93.3 14.7 %collective-permute-start.18 = (bf16[2,2,2,2,64,512]{5,4,3,2,1,0:T(8,128)(2,1)}, bf16[2,2,2,2,64,512]{5,4,3,2,1,0:T(8,128)(2,1)S(1)}, u32[]{:S(2)}, u32[]{:S(2)}) collective-permute-start(bf16[2,2,2,2,64,512]{5,4,3,2,1,0:T(8,128)(2,1)} %get-tuple-element.217), channel_id=1, source_target_pairs={{0,1},{1,0},{2,3},{3,2},{4,5},{5,4},{6,7},{7,6},{8,9},{9,8},{10,11... | collective-permute-start | bytes 3145736 | tf_op jit(solution)/shard_map/ppermute | solution.py:1003
  93.3 14.6 %collective-permute-start.19 = (bf16[2,2,2,2,64,512]{5,4,3,2,1,0:T(8,128)(2,1)}, bf16[2,2,2,2,64,512]{5,4,3,2,1,0:T(8,128)(2,1)S(1)}, u32[]{:S(2)}, u32[]{:S(2)}) collective-permute-start(bf16[2,2,2,2,64,512]{5,4,3,2,1,0:T(8,128)(2,1)} %get-tuple-element.218), channel_id=1, source_target_pairs={{0,1},{1,0},{2,3},{3,2},{4,5},{5,4},{6,7},{7,6},{8,9},{9,8},{10,11... | collective-permute-start | bytes 3145736 | tf_op jit(solution)/shard_map/ppermute | solution.py:1003
  93.8 11.1 %collective-permute-start.16 = (bf16[2,2,96,512]{3,2,1,0:T(8,128)(2,1)S(1)}, bf16[2,2,96,512]{3,2,1,0:T(8,128)(2,1)S(1)}, u32[]{:S(2)}, u32[]{:S(2)}) collective-permute-start(bf16[2,2,96,512]{3,2,1,0:T(8,128)(2,1)S(1)} %get-tuple-element.213.refs_1__0__0_), channel_id=1, source_target_pairs={{0,8},{1,9},{2,10},{3,11},{4,12},{5,13},{6,14},{7,15},{8,0},{9,1},... | collective-permute-start | bytes 1179656 | tf_op jit(solution)/shard_map/ppermute | solution.py:1003
  95.3 10.8 %collective-permute-start.17 = (bf16[2,2,96,512]{3,2,1,0:T(8,128)(2,1)S(1)}, bf16[2,2,96,512]{3,2,1,0:T(8,128)(2,1)S(1)}, u32[]{:S(2)}, u32[]{:S(2)}) collective-permute-start(bf16[2,2,96,512]{3,2,1,0:T(8,128)(2,1)S(1)} %get-tuple-element.214.refs_1__1__0_), channel_id=1, source_target_pairs={{0,16},{1,17},{2,18},{3,19},{4,20},{5,21},{6,22},{7,23},{8,24},{9,... | collective-permute-start | bytes 1179656 | tf_op jit(solution)/shard_map/ppermute | solution.py:1003
  106.8 18.4 %collective-permute-start.20 = (bf16[2,2,2,96,512]{4,3,2,1,0:T(8,128)(2,1)S(1)}, bf16[2,2,2,96,512]{4,3,2,1,0:T(8,128)(2,1)S(1)}, u32[]{:S(2)}, u32[]{:S(2)}) collective-permute-start(bf16[2,2,2,96,512]{4,3,2,1,0:T(8,128)(2,1)S(1)} %get-tuple-element.221.refs_1__0__0_), channel_id=1, source_target_pairs={{0,16},{1,17},{2,18},{3,19},{4,20},{5,21},{6,22},{7,23},{8,24},{9,... | collective-permute-start | bytes 2359304 | tf_op jit(solution)/shard_map/ppermute | solution.py:1003
  107.3 18.1 %collective-permute-start.21 = (bf16[2,2,2,96,512]{4,3,2,1,0:T(8,128)(2,1)S(1)}, bf16[2,2,2,96,512]{4,3,2,1,0:T(8,128)(2,1)S(1)}, u32[]{:S(2)}, u32[]{:S(2)}) collective-permute-start(bf16[2,2,2,96,512]{4,3,2,1,0:T(8,128)(2,1)S(1)} %get-tuple-element.222.refs_1__1__0_), channel_id=1, source_target_pairs={{0,8},{1,9},{2,10},{3,11},{4,12},{5,13},{6,14},{7,15},{8,0},{9,1},... | collective-permute-start | bytes 2359304 | tf_op jit(solution)/shard_map/ppermute | solution.py:1003
  186.7 17.4 %collective-permute-start.24 = (bf16[16,128,512]{2,1,0:T(8,128)(2,1)}, bf16[16,128,512]{2,1,0:T(8,128)(2,1)S(1)}, u32[]{:S(2)}, u32[]{:S(2)}) collective-permute-start(bf16[16,128,512]{2,1,0:T(8,128)(2,1)} %get-tuple-element.235), channel_id=1, source_target_pairs={{0,1},{1,0},{2,3},{3,2},{4,5},{5,4},{6,7},{7,6},{8,9},{9,8},{10,11... | collective-permute-start | bytes 6291464 | tf_op jit(solution)/shard_map/ppermute | solution.py:1003
  186.9 17.1 %collective-permute-start.25 = (bf16[16,64,512]{2,1,0:T(8,128)(2,1)S(1)}, bf16[16,64,512]{2,1,0:T(8,128)(2,1)S(1)}, u32[]{:S(2)}, u32[]{:S(2)}) collective-permute-start(bf16[16,64,512]{2,1,0:T(8,128)(2,1)S(1)} %get-tuple-element.236), channel_id=1, source_target_pairs={{0,1},{1,0},{2,3},{3,2},{4,5},{5,4},{6,7},{7,6},{8,9},{9,8},{10,11... | collective-permute-start | bytes 3145736 | tf_op jit(solution)/shard_map/ppermute | solution.py:1003
  203.8 48.8 %collective-permute-start.30 = (bf16[16,128,512]{2,1,0:T(8,128)(2,1)S(1)}, bf16[16,128,512]{2,1,0:T(8,128)(2,1)S(1)}, u32[]{:S(2)}, u32[]{:S(2)}) collective-permute-start(bf16[16,128,512]{2,1,0:T(8,128)(2,1)S(1)} %get-tuple-element.262), channel_id=1, source_target_pairs={{0,1},{1,0},{2,3},{3,2},{4,5},{5,4},{6,7},{7,6},{8,9},{9,8},{10,11... | collective-permute-start | bytes 6291464 | tf_op jit(solution)/shard_map/ppermute | solution.py:1003
  205.0 19.9 %collective-permute-start.26 = (bf16[768,512]{1,0:T(8,128)(2,1)S(1)}, bf16[768,512]{1,0:T(8,128)(2,1)S(1)}, u32[]{:S(2)}, u32[]{:S(2)}) collective-permute-start(bf16[768,512]{1,0:T(8,128)(2,1)S(1)} %get-tuple-element.244), channel_id=1, source_target_pairs={{0,8},{1,9},{2,10},{3,11},{4,12},{5,13},{6,14},{7,15},{8,0},{9,1},... | collective-permute-start | bytes 2359304 | tf_op jit(solution)/shard_map/ppermute | solution.py:1003
  205.7 19.5 %collective-permute-start.27 = (bf16[768,512]{1,0:T(8,128)(2,1)S(1)}, bf16[768,512]{1,0:T(8,128)(2,1)S(1)}, u32[]{:S(2)}, u32[]{:S(2)}) collective-permute-start(bf16[768,512]{1,0:T(8,128)(2,1)S(1)} %get-tuple-element.246), channel_id=1, source_target_pairs={{0,16},{1,17},{2,18},{3,19},{4,20},{5,21},{6,22},{7,23},{8,24},{9,... | collective-permute-start | bytes 2359304 | tf_op jit(solution)/shard_map/ppermute | solution.py:1003
  234.2 18.8 %collective-permute-start.31 = (bf16[16,16,512]{2,1,0:T(8,128)(2,1)S(1)}, bf16[16,16,512]{2,1,0:T(8,128)(2,1)S(1)}, u32[]{:S(2)}, u32[]{:S(2)}) collective-permute-start(bf16[16,16,512]{2,1,0:T(8,128)(2,1)S(1)} %get-tuple-element.263), channel_id=1, source_target_pairs={{0,1},{1,0},{2,3},{3,2},{4,5},{5,4},{6,7},{7,6},{8,9},{9,8},{10,11... | collective-permute-start | bytes 786440 | tf_op jit(solution)/shard_map/ppermute | solution.py:1003
  234.3 18.8 %collective-permute-start.32 = (bf16[16,16,512]{2,1,0:T(8,128)(2,1)S(1)}, bf16[16,16,512]{2,1,0:T(8,128)(2,1)S(1)}, u32[]{:S(2)}, u32[]{:S(2)}) collective-permute-start(bf16[16,16,512]{2,1,0:T(8,128)(2,1)S(1)} %get-tuple-element.264), channel_id=1, source_target_pairs={{0,1},{1,0},{2,3},{3,2},{4,5},{5,4},{6,7},{7,6},{8,9},{9,8},{10,11... | collective-permute-start | bytes 786440 | tf_op jit(solution)/shard_map/ppermute | solution.py:1003
  236.2 16.8 %collective-permute-start.33 = (bf16[16,16,512]{2,1,0:T(8,128)(2,1)S(1)}, bf16[16,16,512]{2,1,0:T(8,128)(2,1)S(1)}, u32[]{:S(2)}, u32[]{:S(2)}) collective-permute-start(bf16[16,16,512]{2,1,0:T(8,128)(2,1)S(1)} %get-tuple-element.265), channel_id=1, source_target_pairs={{0,1},{1,0},{2,3},{3,2},{4,5},{5,4},{6,7},{7,6},{8,9},{9,8},{10,11... | collective-permute-start | bytes 786440 | tf_op jit(solution)/shard_map/ppermute | solution.py:1003
  237.5 15.6 %collective-permute-start.34 = (bf16[16,16,512]{2,1,0:T(8,128)(2,1)S(1)}, bf16[16,16,512]{2,1,0:T(8,128)(2,1)S(1)}, u32[]{:S(2)}, u32[]{:S(2)}) collective-permute-start(bf16[16,16,512]{2,1,0:T(8,128)(2,1)S(1)} %get-tuple-element.266), channel_id=1, source_target_pairs={{0,1},{1,0},{2,3},{3,2},{4,5},{5,4},{6,7},{7,6},{8,9},{9,8},{10,11... | collective-permute-start | bytes 786440 | tf_op jit(solution)/shard_map/ppermute | solution.py:1003
  252.7 11.6 %collective-permute-start.35 = (bf16[384,512]{1,0:T(8,128)(2,1)S(1)}, bf16[384,512]{1,0:T(8,128)(2,1)S(1)}, u32[]{:S(2)}, u32[]{:S(2)}) collective-permute-start(bf16[384,512]{1,0:T(8,128)(2,1)S(1)} %get-tuple-element.271), channel_id=1, source_target_pairs={{0,2},{1,3},{2,0},{3,1},{4,6},{5,7},{6,4},{7,5},{8,10},{9,11},{10,... | collective-permute-start | bytes 1179656 | tf_op jit(solution)/shard_map/ppermute | solution.py:1003
  254.0 19.7 %collective-permute-start.36 = (bf16[768,512]{1,0:T(8,128)(2,1)S(1)}, bf16[768,512]{1,0:T(8,128)(2,1)S(1)}, u32[]{:S(2)}, u32[]{:S(2)}) collective-permute-start(bf16[768,512]{1,0:T(8,128)(2,1)S(1)} %get-tuple-element.277), channel_id=1, source_target_pairs={{0,8},{1,9},{2,10},{3,11},{4,12},{5,13},{6,14},{7,15},{8,0},{9,1},... | collective-permute-start | bytes 2359304 | tf_op jit(solution)/shard_map/ppermute | solution.py:1003
  255.4 19.4 %collective-permute-start.37 = (bf16[768,512]{1,0:T(8,128)(2,1)S(1)}, bf16[768,512]{1,0:T(8,128)(2,1)S(1)}, u32[]{:S(2)}, u32[]{:S(2)}) collective-permute-start(bf16[768,512]{1,0:T(8,128)(2,1)S(1)} %get-tuple-element.279), channel_id=1, source_target_pairs={{0,16},{1,17},{2,18},{3,19},{4,20},{5,21},{6,22},{7,23},{8,24},{9,... | collective-permute-start | bytes 2359304 | tf_op jit(solution)/shard_map/ppermute | solution.py:1003
  264.9 19.4 %collective-permute-start.38 = (bf16[192,512]{1,0:T(8,128)(2,1)S(1)}, bf16[192,512]{1,0:T(8,128)(2,1)S(1)}, u32[]{:S(2)}, u32[]{:S(2)}) collective-permute-start(bf16[192,512]{1,0:T(8,128)(2,1)S(1)} %get-tuple-element.283), channel_id=1, source_target_pairs={{0,4},{1,5},{2,6},{3,7},{4,0},{5,1},{6,2},{7,3},{8,12},{9,13},{10,... | collective-permute-start | bytes 589832 | tf_op jit(solution)/shard_map/ppermute | solution.py:1003
  276.8 12.0 %collective-permute-start.40 = (bf16[384,512]{1,0:T(8,128)(2,1)}, bf16[384,512]{1,0:T(8,128)(2,1)}, u32[]{:S(2)}, u32[]{:S(2)}) collective-permute-start(bf16[384,512]{1,0:T(8,128)(2,1)} %get-tuple-element.288), channel_id=1, source_target_pairs={{0,8},{1,9},{2,10},{3,11},{4,12},{5,13},{6,14},{7,15},{8,0},{9,1},... | collective-permute-start | bytes 1179656 | tf_op jit(solution)/shard_map/ppermute | solution.py:1003
  290.5 11.1 %collective-permute-start.46 = (bf16[384,512]{1,0:T(8,128)(2,1)S(1)}, bf16[384,512]{1,0:T(8,128)(2,1)S(1)}, u32[]{:S(2)}, u32[]{:S(2)}) collective-permute-start(bf16[384,512]{1,0:T(8,128)(2,1)S(1)} %get-tuple-element.302), channel_id=1, source_target_pairs={{0,2},{1,3},{2,0},{3,1},{4,6},{5,7},{6,4},{7,5},{8,10},{9,11},{10,... | collective-permute-start | bytes 1179656 | tf_op jit(solution)/shard_map/ppermute | solution.py:1003
  304.7 11.2 %collective-permute-start.51 = (bf16[192,512]{1,0:T(8,128)(2,1)S(1)}, bf16[192,512]{1,0:T(8,128)(2,1)S(1)}, u32[]{:S(2)}, u32[]{:S(2)}) collective-permute-start(bf16[192,512]{1,0:T(8,128)(2,1)S(1)} %get-tuple-element.317), channel_id=1, source_target_pairs={{0,4},{1,5},{2,6},{3,7},{4,0},{5,1},{6,2},{7,3},{8,12},{9,13},{10,... | collective-permute-start | bytes 589832 | tf_op jit(solution)/shard_map/ppermute | solution.py:1003
  (53 other events, 516.3 us)
where the time goes:
time: 333 us; the launch traced here: 329 us
  Pallas kernels  197 us (59%)
  waiting for transfers between devices  69.4 us (21%)
  starting transfers between devices  50 us (15%)
  local copies, waits for them, and re-layouts  10.1 us (3%)
    pallas_call x43, Pallas kernels, call(): pl.pallas_call(body, name=name, grid=(steps,), in_specs=[tuple((in_place(...  197 us
    ppermute x54, waiting for transfers between devices, swapped(): lax.ppermute(values, AXES, [(device, device ^ bit) for device in range(SH...  69.4 us
    ppermute x54, starting transfers between devices, swapped(): lax.ppermute(values, AXES, [(device, device ^ bit) for device in range(SH...  50 us
    unnamed x66, local copies, waits for them, and re-layouts  7.53 us
  transfers between devices with their start and end apart: 54, of which 27 were waited for; matrix products, arithmetic and copies ran while one was open for 0% of the time, Pallas kernels for 41%

commit v1 on v0

--- a/solution.py
+++ b/solution.py
@@ -1112,7 +1112,7 @@
                 at = first + block * rows
                 places.append(before + at if at < count // 2 else total // 2 + before + at - count // 2)
             first += rows * blocks
-            flats.append(flat.reshape(-1, 128))
+            flats.extend(stay(flat.reshape(-1, 128)))
             plan.append((rows, blocks, tuple(places)))
             scratch.append(pltpu.VMEM((rows * blocks * 4, 128), F32))
         before += count // 2

time: 333 us -> 330 us (level)
    unnamed x66 -> x44, local copies, waits for them, and re-layouts: 7.53 us -> 4.49 us
where the time goes in v1:
time: 330 us; the launch traced here: 326 us
  Pallas kernels  198 us (60%)
  waiting for transfers between devices  68.4 us (21%)
  starting transfers between devices  50.1 us (15%)
  local copies, waits for them, and re-layouts  7.05 us (2%)
    pallas_call x43, Pallas kernels, call(): pl.pallas_call(body, name=name, grid=(steps,), in_specs=[tuple((in_place(...  198 us
    ppermute x54, waiting for transfers between devices, swapped(): lax.ppermute(values, AXES, [(device, device ^ bit) for device in range(SH...  68.4 us
    ppermute x54, starting transfers between devices, swapped(): lax.ppermute(values, AXES, [(device, device ^ bit) for device in range(SH...  50.1 us
  transfers between devices with their start and end apart: 54, of which 27 were waited for; matrix products, arithmetic and copies ran while one was open for 0% of the time, Pallas kernels for 41%

profile of v1, /device:TPU:0, one launch (start us, length us, event | category | flops | bytes accessed | tf_op | source)
XLA Modules:
  0.0 326.4 jit_solution(15187003937946738083)
XLA Ops:
  2.4 4.1 %collective-permute-start = (bf16[144,512]{1,0:T(8,128)(2,1)S(1)}, bf16[144,512]{1,0:T(8,128)(2,1)S(1)}, u32[]{:S(2)}, u32[]{:S(2)}) collective-permute-start(bf16[144,512]{1,0:T(8,128)(2,1)S(1)} %get-tuple-element.182.refs_1__0__0_), channel_id=1, source_target_pairs={{0,4},{1,5},{2,6},{3,7},{4,0},{5,1},{6,2},{7,3},{8,12},{9,13},{10,... | collective-permute-start | bytes 442376 | tf_op jit(solution)/shard_map/ppermute | solution.py:1003
  9.8 3.8 %collective-permute-done.refs_1__0__1_ = bf16[144,512]{1,0:T(8,128)(2,1)S(1)} collective-permute-done((bf16[144,512]{1,0:T(8,128)(2,1)S(1)}, bf16[144,512]{1,0:T(8,128)(2,1)S(1)}, u32[]{:S(2)}, u32[]{:S(2)}) %collective-permute-start) | collective-permute-done | bytes 147488 | tf_op jit(solution)/shard_map/ppermute | solution.py:1003
  14.9 7.5 %collective-permute-done.1.refs_1__0__1_ = bf16[2,144,512]{2,1,0:T(8,128)(2,1)S(1)} collective-permute-done((bf16[2,144,512]{2,1,0:T(8,128)(2,1)S(1)}, bf16[2,144,512]{2,1,0:T(8,128)(2,1)S(1)}, u32[]{:S(2)}, u32[]{:S(2)}) %collective-permute-start.1) | collective-permute-done | bytes 294944 | tf_op jit(solution)/shard_map/ppermute | solution.py:1003
  25.8 3.3 %collective-permute-start.2 = (bf16[128,512]{1,0:T(8,128)(2,1)S(1)}, bf16[128,512]{1,0:T(8,128)(2,1)S(1)}, u32[]{:S(2)}, u32[]{:S(2)}) collective-permute-start(bf16[128,512]{1,0:T(8,128)(2,1)S(1)} %get-tuple-element.186.refs_1__0__0_), channel_id=1, source_target_pairs={{0,4},{1,5},{2,6},{3,7},{4,0},{5,1},{6,2},{7,3},{8,12},{9,13},{10,... | collective-permute-start | bytes 393224 | tf_op jit(solution)/shard_map/ppermute | solution.py:1003
  29.1 5.4 %collective-permute-done.2.refs_1__0__1_ = bf16[128,512]{1,0:T(8,128)(2,1)S(1)} collective-permute-done((bf16[128,512]{1,0:T(8,128)(2,1)S(1)}, bf16[128,512]{1,0:T(8,128)(2,1)S(1)}, u32[]{:S(2)}, u32[]{:S(2)}) %collective-permute-start.2) | collective-permute-done | bytes 131104 | tf_op jit(solution)/shard_map/ppermute | solution.py:1003
  37.5 6.1 %collective-permute-done.5.refs_1__0__1_ = bf16[2,128,512]{2,1,0:T(8,128)(2,1)S(1)} collective-permute-done((bf16[2,128,512]{2,1,0:T(8,128)(2,1)S(1)}, bf16[2,128,512]{2,1,0:T(8,128)(2,1)S(1)}, u32[]{:S(2)}, u32[]{:S(2)}) %collective-permute-start.5) | collective-permute-done | bytes 262176 | tf_op jit(solution)/shard_map/ppermute | solution.py:1003
  44.2 4.8 %collective-permute-done.6.refs_1__0__1_ = bf16[2,2,2,64,512]{4,3,2,1,0:T(8,128)(2,1)S(1)} collective-permute-done((bf16[2,2,2,64,512]{4,3,2,1,0:T(8,128)(2,1)S(1)}, bf16[2,2,2,64,512]{4,3,2,1,0:T(8,128)(2,1)S(1)}, u32[]{:S(2)}, u32[]{:S(2)}) %collective-permute-start.6) | collective-permute-done | bytes 524320 | tf_op jit(solution)/shard_map/ppermute | solution.py:1003
  49.0 2.6 collective-permute-done.7.refs_1__1__1_
  51.5 2.0 self_0_join_4.1
  58.3 9.8 %project.1 = (bf16[2,512,1536]{2,1,0:T(8,128)(2,1)}, bf16[2,512,1536]{2,1,0:T(8,128)(2,1)}, f32[8,128]{1,0:T(8,128)S(1)}) custom-call(f32[8,128]{1,0:T(8,128)S(1)} %get-tuple-element.195.before_0_, s32[5]{0:T(128)S(1)} %stack.29.refs_0_.refs_2_, bf16[2,512,512]{2,1,0:T(8,128)(2,1)} %refs_2_.7, bf16[2,512,512]{2,1,0:T(8,128)(2,1)} %refs_2_.9, ...), custom_call_target="tpu_custom_call" | custom-call | flops 4600000000 | bytes 65536 | tf_op jit(solution)/shard_map/project/pallas_call | solution.py:757
  69.2 2.5 collective-permute-start.13
  77.5 10.4 %enc_attend.1 = (f32[2,512,512]{2,1,0:T(8,128)}, bf16[2,512,512]{2,1,0:T(8,128)(2,1)}, bf16[2,512,512]{2,1,0:T(8,128)(2,1)}, bf16[2,512,128]{2,1,0:T(8,128)(2,1)}, f32[8,128]{1,0:T(8,128)S(1)}) custom-call(f32[8,128]{1,0:T(8,128)S(1)} %get-tuple-element.203.before_0_, s32[2]{0:T(128)S(1)} %copy-done.12, s32[2,4]{1,0:T(2,128)S(1)} %copy-done.10, ...), custom_call_target="tpu_custom_call" | custom-call | flops 5750000128 | bytes 65536 | tf_op jit(solution)/shard_map/enc_attend/pallas_call | solution.py:757
  88.6 1.9 ffn_0_join_4.1
  93.0 8.3 %dec_attend.1 = (f32[2,512,512]{2,1,0:T(8,128)}, bf16[2,512,512]{2,1,0:T(8,128)(2,1)}, bf16[2,512,512]{2,1,0:T(8,128)(2,1)}, bf16[2,512,128]{2,1,0:T(8,128)(2,1)}, f32[8,128]{1,0:T(8,128)S(1)}) custom-call(f32[8,128]{1,0:T(8,128)S(1)} %get-tuple-element.210.before_0_, s32[2]{0:T(128)S(1)} %copy-done.12, s32[2,4]{1,0:T(2,128)S(1)} %copy-done.11, ...), custom_call_target="tpu_custom_call" | custom-call | flops 5750000128 | bytes 65536 | tf_op jit(solution)/shard_map/dec_attend/pallas_call | solution.py:757
  105.1 15.1 %ffn_forward.1 = (bf16[2,512,512]{2,1,0:T(8,128)(2,1)}, bf16[2,512,2048]{2,1,0:T(8,128)(2,1)}, bf16[2,512,2048]{2,1,0:T(8,128)(2,1)}, f32[8,128]{1,0:T(8,128)S(1)}) custom-call(f32[8,128]{1,0:T(8,128)S(1)} %get-tuple-element.215.before_0_, s32[5]{0:T(128)S(1)} %stack.29.refs_0_.refs_2_, f32[2,512,512]{2,1,0:T(8,128)} %get-tuple-element.216.refs_1_.refs_2_, ...), custom_call_target="tpu_custom_call" | custom-call | flops 9200000000 | bytes 65536 | tf_op jit(solution)/shard_map/ffn_forward/pallas_call | solution.py:757
  120.2 2.1 collective-permute-done.20.refs_1__0__1_
  122.6 2.3 late_0_join_4.1
  125.5 3.1 collective-permute-done.22
  128.6 2.2 collective-permute-done.23
  132.0 51.9 %upper_decoder.1 = (bf16[2,512,512]{2,1,0:T(8,128)(2,1)}, f32[2,512,512]{2,1,0:T(8,128)}, f32[2,512,512]{2,1,0:T(8,128)}, bf16[16,128,512]{2,1,0:T(8,128)(2,1)},...) custom-call(f32[8,128]{1,0:T(8,128)S(1)} %get-tuple-element.223.befo, ...), custom_call_target="tpu_custom_call" | custom-call | flops 34500001792 | bytes 65536 | tf_op jit(solution)/shard_map/upper_decoder/pallas_call | solution.py:757
  184.5 16.5 %ffn_backward.1 = (f32[2,512,512]{2,1,0:T(8,128)S(1)}, bf16[16,128,512]{2,1,0:T(8,128)(2,1)S(1)}, bf16[16,128,512]{2,1,0:T(8,128)(2,1)S(1)}, f32[8,512]{1,0:T(8,128)S(1)}, f32[8,128]{1,0:T(8,128)S(1)}) custom-call(f32[8,128]{1,0:T(8,128)S(1)} %get-tuple-element.228.before_0_, s32[5]{0:T(128)S(1)} %stack.29.refs_0_.refs_2_, ...), custom_call_target="tpu_custom_call" | custom-call | flops 12650000384 | bytes 65536 | tf_op jit(solution)/shard_map/ffn_backward/pallas_call | solution.py:757
  204.4 17.3 %enc_attend_back.1 = (bf16[2,512,1536]{2,1,0:T(8,128)(2,1)S(1)}, f32[8,128]{1,0:T(8,128)S(1)}) custom-call(f32[8,128]{1,0:T(8,128)S(1)} %get-tuple-element.237.before_0_, s32[2]{0:T(128)S(1)} %copy-done.12, s32[2,4]{1,0:T(2,128)S(1)} %copy-done.10, s32[5]{0:T(128)S(1)} %stack.29.refs_0_.refs_2_, f32[2,512,512]{2,1,0:T(8,128)S(1)} %get-tuple-element.238.refs_3_.refs_1_, ...), custom_call_target="tpu_custom_call" | custom-call | flops 9200000000 | bytes 65536 | tf_op jit(solution)/shard_map/enc_attend_back/pallas_call | solution.py:757
  226.1 5.3 %enc_self_weights.1 = (bf16[16,64,512]{2,1,0:T(8,128)(2,1)S(1)}, bf16[16,16,512]{2,1,0:T(8,128)(2,1)S(1)}, bf16[16,16,512]{2,1,0:T(8,128)(2,1)S(1)}, bf16[16,16,...) custom-call(f32[8,128]{1,0:T(8,128)S(1)} %get-tuple-element.247.before_0_, ...), custom_call_target="tpu_custom_call" | custom-call | flops 4600000000 | bytes 65536 | tf_op jit(solution)/shard_map/enc_self_weights/pallas_call | solution.py:757
  234.7 14.3 %dec_attend_back.1 = (bf16[2,512,1536]{2,1,0:T(8,128)(2,1)S(1)}, f32[8,128]{1,0:T(8,128)S(1)}) custom-call(f32[8,128]{1,0:T(8,128)S(1)} %get-tuple-element.249.before_0_, s32[2]{0:T(128)S(1)} %copy-done.12, s32[2,4]{1,0:T(2,128)S(1)} %copy-done.11, s32[5]{0:T(128)S(1)} %stack.29.refs_0_.refs_2_, f32[2,512,512]{2,1,0:T(8,128)S(1)} %copy-done.13, ...), custom_call_target="tpu_custom_call" | custom-call | flops 9200000000 | bytes 65536 | tf_op jit(solution)/shard_map/dec_attend_back/pallas_call | solution.py:757
  253.2 6.5 %enc_self_rows.1 = (bf16[2,512,512]{2,1,0:T(8,128)(2,1)}, f32[8,512]{1,0:T(8,128)S(1)}, f32[8,128]{1,0:T(8,128)S(1)}) custom-call(f32[8,128]{1,0:T(8,128)S(1)} %get-tuple-element.267.before_0_, s32[5]{0:T(128)S(1)} %stack.29.refs_0_.refs_2_, f32[2,512,512]{2,1,0:T(8,128)} %copy-done.15, bf16[2,512,512]{2,1,0:T(8,128)(2,1)} %refs_2_.7, ...), custom_call_target="tpu_custom_call" | custom-call | flops 4024999936 | bytes 65536 | tf_op jit(solution)/shard_map/enc_self_rows/pallas_call | solution.py:757
  263.5 6.4 %dec_self_rows.1 = (bf16[2,512,512]{2,1,0:T(8,128)(2,1)}, f32[8,512]{1,0:T(8,128)S(1)}, f32[8,128]{1,0:T(8,128)S(1)}) custom-call(f32[8,128]{1,0:T(8,128)S(1)} %get-tuple-element.272.before_0_, s32[5]{0:T(128)S(1)} %stack.29.refs_0_.refs_2_, f32[2,512,512]{2,1,0:T(8,128)} %get-tuple-element.250.refs_3_.refs_1_, bf16[2,512,512]{2,1,0:T(8,128)(2,1)} %refs_2_.9, ...), custom_call_target="tpu_custom_call" | custom-call | flops 4024999936 | bytes 65536 | tf_op jit(solution)/shard_map/dec_self_rows/pallas_call | solution.py:757
  274.5 6.2 %dec_self_weights.1 = (bf16[16,64,512]{2,1,0:T(8,128)(2,1)S(1)}, bf16[16,16,512]{2,1,0:T(8,128)(2,1)}, bf16[16,16,512]{2,1,0:T(8,128)(2,1)}, bf16[16,16,512]{2,1...) custom-call(f32[8,128]{1,0:T(8,128)S(1)} %get-tuple-element.280.before_0_, ...), custom_call_target="tpu_custom_call" | custom-call | flops 4600000000 | bytes 65536 | tf_op jit(solution)/shard_map/dec_self_weights/pallas_call | solution.py:757
  287.4 1.8 collective-permute-start.46
  291.4 7.1 %collective-permute-done.46.refs_2_ = bf16[384,512]{1,0:T(8,128)(2,1)S(1)} collective-permute-done((bf16[384,512]{1,0:T(8,128)(2,1)S(1)}, bf16[384,512]{1,0:T(8,128)(2,1)S(1)}, u32[]{:S(2)}, u32[]{:S(2)}) %collective-permute-start.46) | collective-permute-done | bytes 393248 | tf_op jit(solution)/shard_map/ppermute | solution.py:1003
  307.8 5.1 %collective-permute-done.51.refs_1__1_ = bf16[192,512]{1,0:T(8,128)(2,1)S(1)} collective-permute-done((bf16[192,512]{1,0:T(8,128)(2,1)S(1)}, bf16[192,512]{1,0:T(8,128)(2,1)S(1)}, u32[]{:S(2)}, u32[]{:S(2)}) %collective-permute-start.51) | collective-permute-done | bytes 196640 | tf_op jit(solution)/shard_map/ppermute | solution.py:1003
  314.9 2.3 collective-permute-start.53
  317.2 5.9 %collective-permute-done.53.refs_1__1_ = bf16[112,512]{1,0:T(8,128)(2,1)S(1)} collective-permute-done((bf16[112,512]{1,0:T(8,128)(2,1)S(1)}, bf16[112,512]{1,0:T(8,128)(2,1)S(1)}, u32[]{:S(2)}, u32[]{:S(2)}) %collective-permute-start.53) | collective-permute-done | bytes 114720 | tf_op jit(solution)/shard_map/ppermute | solution.py:1003
  (186 shorter events, 80.8 us)
Async XLA Ops:
  2.4 11.1 %collective-permute-start = (bf16[144,512]{1,0:T(8,128)(2,1)S(1)}, bf16[144,512]{1,0:T(8,128)(2,1)S(1)}, u32[]{:S(2)}, u32[]{:S(2)}) collective-permute-start(bf16[144,512]{1,0:T(8,128)(2,1)S(1)} %get-tuple-element.182.refs_1__0__0_), channel_id=1, source_target_pairs={{0,4},{1,5},{2,6},{3,7},{4,0},{5,1},{6,2},{7,3},{8,12},{9,13},{10,... | collective-permute-start | bytes 442376 | tf_op jit(solution)/shard_map/ppermute | solution.py:1003
  22.9 12.2 %collective-permute-start.4 = (bf16[2,2,80,512]{3,2,1,0:T(8,128)(2,1)S(1)}, bf16[2,2,80,512]{3,2,1,0:T(8,128)(2,1)S(1)}, u32[]{:S(2)}, u32[]{:S(2)}) collective-permute-start(bf16[2,2,80,512]{3,2,1,0:T(8,128)(2,1)S(1)} %get-tuple-element.189.refs_1__1__0_), channel_id=1, source_target_pairs={{0,16},{1,17},{2,18},{3,19},{4,20},{5,21},{6,22},{7,23},{8,24},{9,... | collective-permute-start | bytes 983048 | tf_op jit(solution)/shard_map/ppermute | solution.py:1003
  35.7 15.8 %collective-permute-start.7 = (bf16[2,2,2,80,512]{4,3,2,1,0:T(8,128)(2,1)S(1)}, bf16[2,2,2,80,512]{4,3,2,1,0:T(8,128)(2,1)S(1)}, u32[]{:S(2)}, u32[]{:S(2)}) collective-permute-start(bf16[2,2,2,80,512]{4,3,2,1,0:T(8,128)(2,1)S(1)} %get-tuple-element.194.refs_1__1__0_), channel_id=1, source_target_pairs={{0,8},{1,9},{2,10},{3,11},{4,12},{5,13},{6,14},{7,15},{8,0},{9,1},... | collective-permute-start | bytes 1966088 | tf_op jit(solution)/shard_map/ppermute | solution.py:1003
  36.3 12.6 %collective-permute-start.6 = (bf16[2,2,2,64,512]{4,3,2,1,0:T(8,128)(2,1)S(1)}, bf16[2,2,2,64,512]{4,3,2,1,0:T(8,128)(2,1)S(1)}, u32[]{:S(2)}, u32[]{:S(2)}) collective-permute-start(bf16[2,2,2,64,512]{4,3,2,1,0:T(8,128)(2,1)S(1)} %get-tuple-element.193.refs_1__0__0_), channel_id=1, source_target_pairs={{0,16},{1,17},{2,18},{3,19},{4,20},{5,21},{6,22},{7,23},{8,24},{9,... | collective-permute-start | bytes 1572872 | tf_op jit(solution)/shard_map/ppermute | solution.py:1003
  54.1 14.1 %collective-permute-start.10 = (bf16[192,512]{1,0:T(8,128)(2,1)S(1)}, bf16[192,512]{1,0:T(8,128)(2,1)}, u32[]{:S(2)}, u32[]{:S(2)}) collective-permute-start(bf16[192,512]{1,0:T(8,128)(2,1)S(1)} %get-tuple-element.199.refs_1__0__0_), channel_id=1, source_target_pairs={{0,4},{1,5},{2,6},{3,7},{4,0},{5,1},{6,2},{7,3},{8,12},{9,13},{10,... | collective-permute-start | bytes 589832 | tf_op jit(solution)/shard_map/ppermute | solution.py:1003
  54.1 17.7 %collective-permute-start.11 = (bf16[2,2,64,512]{3,2,1,0:T(8,128)(2,1)S(1)}, bf16[2,2,64,512]{3,2,1,0:T(8,128)(2,1)S(1)}, u32[]{:S(2)}, u32[]{:S(2)}) collective-permute-start(bf16[2,2,64,512]{3,2,1,0:T(8,128)(2,1)S(1)} %get-tuple-element.201.refs_1__0__0_), channel_id=1, source_target_pairs={{0,8},{1,9},{2,10},{3,11},{4,12},{5,13},{6,14},{7,15},{8,0},{9,1},... | collective-permute-start | bytes 786440 | tf_op jit(solution)/shard_map/ppermute | solution.py:1003
  55.1 17.3 %collective-permute-start.12 = (bf16[2,2,64,512]{3,2,1,0:T(8,128)(2,1)S(1)}, bf16[2,2,64,512]{3,2,1,0:T(8,128)(2,1)}, u32[]{:S(2)}, u32[]{:S(2)}) collective-permute-start(bf16[2,2,64,512]{3,2,1,0:T(8,128)(2,1)S(1)} %get-tuple-element.202.refs_1__1__0_), channel_id=1, source_target_pairs={{0,16},{1,17},{2,18},{3,19},{4,20},{5,21},{6,22},{7,23},{8,24},{9,... | collective-permute-start | bytes 786440 | tf_op jit(solution)/shard_map/ppermute | solution.py:1003
  69.2 18.7 %collective-permute-start.13 = (bf16[2,192,512]{2,1,0:T(8,128)(2,1)S(1)}, bf16[2,192,512]{2,1,0:T(8,128)(2,1)S(1)}, u32[]{:S(2)}, u32[]{:S(2)}) collective-permute-start(bf16[2,192,512]{2,1,0:T(8,128)(2,1)S(1)} %get-tuple-element.206.refs_1__0__0_), channel_id=1, source_target_pairs={{0,2},{1,3},{2,0},{3,1},{4,6},{5,7},{6,4},{7,5},{8,10},{9,11},{10,... | collective-permute-start | bytes 1179656 | tf_op jit(solution)/shard_map/ppermute | solution.py:1003
  74.5 14.1 %collective-permute-start.14 = (bf16[2,2,2,64,512]{4,3,2,1,0:T(8,128)(2,1)S(1)}, bf16[2,2,2,64,512]{4,3,2,1,0:T(8,128)(2,1)S(1)}, u32[]{:S(2)}, u32[]{:S(2)}) collective-permute-start(bf16[2,2,2,64,512]{4,3,2,1,0:T(8,128)(2,1)S(1)} %get-tuple-element.208.refs_1__0__0_), channel_id=1, source_target_pairs={{0,16},{1,17},{2,18},{3,19},{4,20},{5,21},{6,22},{7,23},{8,24},{9,... | collective-permute-start | bytes 1572872 | tf_op jit(solution)/shard_map/ppermute | solution.py:1003
  76.0 12.5 %collective-permute-start.15 = (bf16[2,2,2,64,512]{4,3,2,1,0:T(8,128)(2,1)S(1)}, bf16[2,2,2,64,512]{4,3,2,1,0:T(8,128)(2,1)S(1)}, u32[]{:S(2)}, u32[]{:S(2)}) collective-permute-start(bf16[2,2,2,64,512]{4,3,2,1,0:T(8,128)(2,1)S(1)} %get-tuple-element.209.refs_1__1__0_), channel_id=1, source_target_pairs={{0,8},{1,9},{2,10},{3,11},{4,12},{5,13},{6,14},{7,15},{8,0},{9,1},... | collective-permute-start | bytes 1572872 | tf_op jit(solution)/shard_map/ppermute | solution.py:1003
  90.4 14.7 %collective-permute-start.18 = (bf16[2,2,2,2,64,512]{5,4,3,2,1,0:T(8,128)(2,1)}, bf16[2,2,2,2,64,512]{5,4,3,2,1,0:T(8,128)(2,1)S(1)}, u32[]{:S(2)}, u32[]{:S(2)}) collective-permute-start(bf16[2,2,2,2,64,512]{5,4,3,2,1,0:T(8,128)(2,1)} %get-tuple-element.217), channel_id=1, source_target_pairs={{0,1},{1,0},{2,3},{3,2},{4,5},{5,4},{6,7},{7,6},{8,9},{9,8},{10,11... | collective-permute-start | bytes 3145736 | tf_op jit(solution)/shard_map/ppermute | solution.py:1003
  90.5 14.6 %collective-permute-start.19 = (bf16[2,2,2,2,64,512]{5,4,3,2,1,0:T(8,128)(2,1)}, bf16[2,2,2,2,64,512]{5,4,3,2,1,0:T(8,128)(2,1)S(1)}, u32[]{:S(2)}, u32[]{:S(2)}) collective-permute-start(bf16[2,2,2,2,64,512]{5,4,3,2,1,0:T(8,128)(2,1)} %get-tuple-element.218), channel_id=1, source_target_pairs={{0,1},{1,0},{2,3},{3,2},{4,5},{5,4},{6,7},{7,6},{8,9},{9,8},{10,11... | collective-permute-start | bytes 3145736 | tf_op jit(solution)/shard_map/ppermute | solution.py:1003
  91.0 11.1 %collective-permute-start.16 = (bf16[2,2,96,512]{3,2,1,0:T(8,128)(2,1)S(1)}, bf16[2,2,96,512]{3,2,1,0:T(8,128)(2,1)S(1)}, u32[]{:S(2)}, u32[]{:S(2)}) collective-permute-start(bf16[2,2,96,512]{3,2,1,0:T(8,128)(2,1)S(1)} %get-tuple-element.213.refs_1__0__0_), channel_id=1, source_target_pairs={{0,8},{1,9},{2,10},{3,11},{4,12},{5,13},{6,14},{7,15},{8,0},{9,1},... | collective-permute-start | bytes 1179656 | tf_op jit(solution)/shard_map/ppermute | solution.py:1003
  92.5 10.8 %collective-permute-start.17 = (bf16[2,2,96,512]{3,2,1,0:T(8,128)(2,1)S(1)}, bf16[2,2,96,512]{3,2,1,0:T(8,128)(2,1)S(1)}, u32[]{:S(2)}, u32[]{:S(2)}) collective-permute-start(bf16[2,2,96,512]{3,2,1,0:T(8,128)(2,1)S(1)} %get-tuple-element.214.refs_1__1__0_), channel_id=1, source_target_pairs={{0,16},{1,17},{2,18},{3,19},{4,20},{5,21},{6,22},{7,23},{8,24},{9,... | collective-permute-start | bytes 1179656 | tf_op jit(solution)/shard_map/ppermute | solution.py:1003
  103.9 18.4 %collective-permute-start.20 = (bf16[2,2,2,96,512]{4,3,2,1,0:T(8,128)(2,1)S(1)}, bf16[2,2,2,96,512]{4,3,2,1,0:T(8,128)(2,1)S(1)}, u32[]{:S(2)}, u32[]{:S(2)}) collective-permute-start(bf16[2,2,2,96,512]{4,3,2,1,0:T(8,128)(2,1)S(1)} %get-tuple-element.221.refs_1__0__0_), channel_id=1, source_target_pairs={{0,16},{1,17},{2,18},{3,19},{4,20},{5,21},{6,22},{7,23},{8,24},{9,... | collective-permute-start | bytes 2359304 | tf_op jit(solution)/shard_map/ppermute | solution.py:1003
  104.5 18.1 %collective-permute-start.21 = (bf16[2,2,2,96,512]{4,3,2,1,0:T(8,128)(2,1)S(1)}, bf16[2,2,2,96,512]{4,3,2,1,0:T(8,128)(2,1)S(1)}, u32[]{:S(2)}, u32[]{:S(2)}) collective-permute-start(bf16[2,2,2,96,512]{4,3,2,1,0:T(8,128)(2,1)S(1)} %get-tuple-element.222.refs_1__1__0_), channel_id=1, source_target_pairs={{0,8},{1,9},{2,10},{3,11},{4,12},{5,13},{6,14},{7,15},{8,0},{9,1},... | collective-permute-start | bytes 2359304 | tf_op jit(solution)/shard_map/ppermute | solution.py:1003
  183.9 17.3 %collective-permute-start.24 = (bf16[16,128,512]{2,1,0:T(8,128)(2,1)}, bf16[16,128,512]{2,1,0:T(8,128)(2,1)S(1)}, u32[]{:S(2)}, u32[]{:S(2)}) collective-permute-start(bf16[16,128,512]{2,1,0:T(8,128)(2,1)} %get-tuple-element.235), channel_id=1, source_target_pairs={{0,1},{1,0},{2,3},{3,2},{4,5},{5,4},{6,7},{7,6},{8,9},{9,8},{10,11... | collective-permute-start | bytes 6291464 | tf_op jit(solution)/shard_map/ppermute | solution.py:1003
  184.1 17.1 %collective-permute-start.25 = (bf16[16,64,512]{2,1,0:T(8,128)(2,1)S(1)}, bf16[16,64,512]{2,1,0:T(8,128)(2,1)S(1)}, u32[]{:S(2)}, u32[]{:S(2)}) collective-permute-start(bf16[16,64,512]{2,1,0:T(8,128)(2,1)S(1)} %get-tuple-element.236), channel_id=1, source_target_pairs={{0,1},{1,0},{2,3},{3,2},{4,5},{5,4},{6,7},{7,6},{8,9},{9,8},{10,11... | collective-permute-start | bytes 3145736 | tf_op jit(solution)/shard_map/ppermute | solution.py:1003
  201.1 48.6 %collective-permute-start.30 = (bf16[16,128,512]{2,1,0:T(8,128)(2,1)S(1)}, bf16[16,128,512]{2,1,0:T(8,128)(2,1)S(1)}, u32[]{:S(2)}, u32[]{:S(2)}) collective-permute-start(bf16[16,128,512]{2,1,0:T(8,128)(2,1)S(1)} %get-tuple-element.262), channel_id=1, source_target_pairs={{0,1},{1,0},{2,3},{3,2},{4,5},{5,4},{6,7},{7,6},{8,9},{9,8},{10,11... | collective-permute-start | bytes 6291464 | tf_op jit(solution)/shard_map/ppermute | solution.py:1003
  202.2 19.9 %collective-permute-start.26 = (bf16[768,512]{1,0:T(8,128)(2,1)S(1)}, bf16[768,512]{1,0:T(8,128)(2,1)S(1)}, u32[]{:S(2)}, u32[]{:S(2)}) collective-permute-start(bf16[768,512]{1,0:T(8,128)(2,1)S(1)} %get-tuple-element.244), channel_id=1, source_target_pairs={{0,8},{1,9},{2,10},{3,11},{4,12},{5,13},{6,14},{7,15},{8,0},{9,1},... | collective-permute-start | bytes 2359304 | tf_op jit(solution)/shard_map/ppermute | solution.py:1003
  202.9 19.5 %collective-permute-start.27 = (bf16[768,512]{1,0:T(8,128)(2,1)S(1)}, bf16[768,512]{1,0:T(8,128)(2,1)S(1)}, u32[]{:S(2)}, u32[]{:S(2)}) collective-permute-start(bf16[768,512]{1,0:T(8,128)(2,1)S(1)} %get-tuple-element.246), channel_id=1, source_target_pairs={{0,16},{1,17},{2,18},{3,19},{4,20},{5,21},{6,22},{7,23},{8,24},{9,... | collective-permute-start | bytes 2359304 | tf_op jit(solution)/shard_map/ppermute | solution.py:1003
  231.4 18.7 %collective-permute-start.31 = (bf16[16,16,512]{2,1,0:T(8,128)(2,1)S(1)}, bf16[16,16,512]{2,1,0:T(8,128)(2,1)S(1)}, u32[]{:S(2)}, u32[]{:S(2)}) collective-permute-start(bf16[16,16,512]{2,1,0:T(8,128)(2,1)S(1)} %get-tuple-element.263), channel_id=1, source_target_pairs={{0,1},{1,0},{2,3},{3,2},{4,5},{5,4},{6,7},{7,6},{8,9},{9,8},{10,11... | collective-permute-start | bytes 786440 | tf_op jit(solution)/shard_map/ppermute | solution.py:1003
  231.5 18.6 %collective-permute-start.32 = (bf16[16,16,512]{2,1,0:T(8,128)(2,1)S(1)}, bf16[16,16,512]{2,1,0:T(8,128)(2,1)S(1)}, u32[]{:S(2)}, u32[]{:S(2)}) collective-permute-start(bf16[16,16,512]{2,1,0:T(8,128)(2,1)S(1)} %get-tuple-element.264), channel_id=1, source_target_pairs={{0,1},{1,0},{2,3},{3,2},{4,5},{5,4},{6,7},{7,6},{8,9},{9,8},{10,11... | collective-permute-start | bytes 786440 | tf_op jit(solution)/shard_map/ppermute | solution.py:1003
  233.4 16.6 %collective-permute-start.33 = (bf16[16,16,512]{2,1,0:T(8,128)(2,1)S(1)}, bf16[16,16,512]{2,1,0:T(8,128)(2,1)S(1)}, u32[]{:S(2)}, u32[]{:S(2)}) collective-permute-start(bf16[16,16,512]{2,1,0:T(8,128)(2,1)S(1)} %get-tuple-element.265), channel_id=1, source_target_pairs={{0,1},{1,0},{2,3},{3,2},{4,5},{5,4},{6,7},{7,6},{8,9},{9,8},{10,11... | collective-permute-start | bytes 786440 | tf_op jit(solution)/shard_map/ppermute | solution.py:1003
  234.6 15.4 %collective-permute-start.34 = (bf16[16,16,512]{2,1,0:T(8,128)(2,1)S(1)}, bf16[16,16,512]{2,1,0:T(8,128)(2,1)S(1)}, u32[]{:S(2)}, u32[]{:S(2)}) collective-permute-start(bf16[16,16,512]{2,1,0:T(8,128)(2,1)S(1)} %get-tuple-element.266), channel_id=1, source_target_pairs={{0,1},{1,0},{2,3},{3,2},{4,5},{5,4},{6,7},{7,6},{8,9},{9,8},{10,11... | collective-permute-start | bytes 786440 | tf_op jit(solution)/shard_map/ppermute | solution.py:1003
  249.7 11.6 %collective-permute-start.35 = (bf16[384,512]{1,0:T(8,128)(2,1)S(1)}, bf16[384,512]{1,0:T(8,128)(2,1)S(1)}, u32[]{:S(2)}, u32[]{:S(2)}) collective-permute-start(bf16[384,512]{1,0:T(8,128)(2,1)S(1)} %get-tuple-element.271), channel_id=1, source_target_pairs={{0,2},{1,3},{2,0},{3,1},{4,6},{5,7},{6,4},{7,5},{8,10},{9,11},{10,... | collective-permute-start | bytes 1179656 | tf_op jit(solution)/shard_map/ppermute | solution.py:1003
  250.9 19.8 %collective-permute-start.36 = (bf16[768,512]{1,0:T(8,128)(2,1)S(1)}, bf16[768,512]{1,0:T(8,128)(2,1)S(1)}, u32[]{:S(2)}, u32[]{:S(2)}) collective-permute-start(bf16[768,512]{1,0:T(8,128)(2,1)S(1)} %get-tuple-element.277), channel_id=1, source_target_pairs={{0,8},{1,9},{2,10},{3,11},{4,12},{5,13},{6,14},{7,15},{8,0},{9,1},... | collective-permute-start | bytes 2359304 | tf_op jit(solution)/shard_map/ppermute | solution.py:1003
  252.5 19.4 %collective-permute-start.37 = (bf16[768,512]{1,0:T(8,128)(2,1)S(1)}, bf16[768,512]{1,0:T(8,128)(2,1)S(1)}, u32[]{:S(2)}, u32[]{:S(2)}) collective-permute-start(bf16[768,512]{1,0:T(8,128)(2,1)S(1)} %get-tuple-element.279), channel_id=1, source_target_pairs={{0,16},{1,17},{2,18},{3,19},{4,20},{5,21},{6,22},{7,23},{8,24},{9,... | collective-permute-start | bytes 2359304 | tf_op jit(solution)/shard_map/ppermute | solution.py:1003
  261.9 19.4 %collective-permute-start.38 = (bf16[192,512]{1,0:T(8,128)(2,1)S(1)}, bf16[192,512]{1,0:T(8,128)(2,1)S(1)}, u32[]{:S(2)}, u32[]{:S(2)}) collective-permute-start(bf16[192,512]{1,0:T(8,128)(2,1)S(1)} %get-tuple-element.283), channel_id=1, source_target_pairs={{0,4},{1,5},{2,6},{3,7},{4,0},{5,1},{6,2},{7,3},{8,12},{9,13},{10,... | collective-permute-start | bytes 589832 | tf_op jit(solution)/shard_map/ppermute | solution.py:1003
  273.9 11.9 %collective-permute-start.40 = (bf16[384,512]{1,0:T(8,128)(2,1)}, bf16[384,512]{1,0:T(8,128)(2,1)}, u32[]{:S(2)}, u32[]{:S(2)}) collective-permute-start(bf16[384,512]{1,0:T(8,128)(2,1)} %get-tuple-element.288), channel_id=1, source_target_pairs={{0,8},{1,9},{2,10},{3,11},{4,12},{5,13},{6,14},{7,15},{8,0},{9,1},... | collective-permute-start | bytes 1179656 | tf_op jit(solution)/shard_map/ppermute | solution.py:1003
  287.4 11.1 %collective-permute-start.46 = (bf16[384,512]{1,0:T(8,128)(2,1)S(1)}, bf16[384,512]{1,0:T(8,128)(2,1)S(1)}, u32[]{:S(2)}, u32[]{:S(2)}) collective-permute-start(bf16[384,512]{1,0:T(8,128)(2,1)S(1)} %get-tuple-element.302), channel_id=1, source_target_pairs={{0,2},{1,3},{2,0},{3,1},{4,6},{5,7},{6,4},{7,5},{8,10},{9,11},{10,... | collective-permute-start | bytes 1179656 | tf_op jit(solution)/shard_map/ppermute | solution.py:1003
  301.7 11.2 %collective-permute-start.51 = (bf16[192,512]{1,0:T(8,128)(2,1)S(1)}, bf16[192,512]{1,0:T(8,128)(2,1)S(1)}, u32[]{:S(2)}, u32[]{:S(2)}) collective-permute-start(bf16[192,512]{1,0:T(8,128)(2,1)S(1)} %get-tuple-element.317), channel_id=1, source_target_pairs={{0,4},{1,5},{2,6},{3,7},{4,0},{5,1},{6,2},{7,3},{8,12},{9,13},{10,... | collective-permute-start | bytes 589832 | tf_op jit(solution)/shard_map/ppermute | solution.py:1003
  (42 other events, 470.9 us)
